TPU v7x, 32 devices: a whole 2x2x4 slice. The times are simulated.
32 devices in a mesh: seq: 8 (over y, x, core), shard: 4 (over z).
Axes of the slice: x: 2, y: 2, z: 4, core: 2. Of those that a mesh axis runs over, the one named last changes fastest.
Arguments:
- tokens: bfloat16 [40960, 768], P(('seq', 'shard')), may hold values from -6 to 6
- positions: int32 [40960], P(('seq', 'shard')), may hold values from 0 to 2430, as said below
- cotangent: bfloat16 [40960, 768], P(('seq', 'shard')), may hold values from -6 to 6
- qkv_weight: float32 [768, 2304], P('shard'), may hold values from -0.21875 to 0.21875
- attn_weight: float32 [768, 768], P('shard'), may hold values from -0.875 to 0.875
- mlp_weight: float32 [768, 2304], P('shard'), may hold values from -0.21875 to 0.21875
- down_weight: float32 [1152, 768], P('shard'), may hold values from -0.1875 to 0.1875
- norm_gains: float32 [2, 768], P(None, 'shard'), may hold values from 0.5 to 1.5
- qkv_first: float32 [768, 2304], P('shard'), may hold values from -64 to 64
- qkv_second: float32 [768, 2304], P('shard'), may hold values from 208.896 to 835.584
- attn_first: float32 [768, 768], P('shard'), may hold values from -32 to 32
- attn_second: float32 [768, 768], P('shard'), may hold values from 52.224 to 208.896
- mlp_first: float32 [768, 2304], P('shard'), may hold values from -64 to 64
- mlp_second: float32 [768, 2304], P('shard'), may hold values from 169.1648 to 676.6592
- down_first: float32 [1152, 768], P('shard'), may hold values from -80 to 80
- down_second: float32 [1152, 768], P('shard'), may hold values from 300.6464 to 1203.4048
- gains_first: float32 [2, 768], P(None, 'shard'), may hold values from -112 to 112
- gains_second: float32 [2, 768], P(None, 'shard'), may hold values from 534.9376 to 2139.7505
Outputs:
- layer_output: bfloat16 [40960, 768], P(('seq', 'shard'))
- input_grad: bfloat16 [40960, 768], P(('seq', 'shard'))
- qkv_first_new: float32 [768, 2304], P('shard')
- qkv_second_new: float32 [768, 2304], P('shard')
- qkv_new: float32 [768, 2304], P('shard')
- attn_first_new: float32 [768, 768], P('shard')
- attn_second_new: float32 [768, 768], P('shard')
- attn_new: float32 [768, 768], P('shard')
- mlp_first_new: float32 [768, 2304], P('shard')
- mlp_second_new: float32 [768, 2304], P('shard')
- mlp_new: float32 [768, 2304], P('shard')
- down_first_new: float32 [1152, 768], P('shard')
- down_second_new: float32 [1152, 768], P('shard')
- down_new: float32 [1152, 768], P('shard')
- gains_first_new: float32 [2, 768], P(None, 'shard')
- gains_second_new: float32 [2, 768], P(None, 'shard')
- gains_new: float32 [2, 768], P(None, 'shard')
Inputs may be any that keep to these rules, and one draw needn't show every extreme that they name: positions[t] counts the tokens of t's document before t. A document starts at token 0, and exactly once in each aligned run of 1280 tokens (the tokens of one device), never among the first 64 or the last 64 tokens of that run.
All inputs are finite; a program needn't handle non-finite values.
Results may differ from a plain program's by a relative error of at most 0.015.
Values may be sent and summed in bfloat16 or wider, within the bound.
No kernel may reach another device: no remote copies, remote signals or barrier semaphores. Data moves between devices by JAX's collectives and lax.ppermute only.
A program may use at most 320 MiB of HBM per device.

v0:
```python
import functools
import math

import jax
import jax.numpy as jnp
from jax import lax
from jax.experimental import pallas as pl
from jax.experimental.pallas import tpu as pltpu
from jax.sharding import PartitionSpec as P

HEADS = 12
HALF = 64
ADAM_STEP = 5
LANES = 128
ROWS = 64
SPAN = ROWS + 2 * HALF
PAIR = 2 * ROWS
TILE = 256
WIDE_TILE = 640


norm_epsilon = 1e-05
rope_theta = 10000.0
beta_first = 0.9
beta_second = 0.98
adam_epsilon = 1e-06
decay_rate = 1e-05
rate_matrix = 0.04
rate_gains = 0.2
masked_score = -1e30
vmem_bytes = 60 * 1024 * 1024

f32 = jnp.float32
bf16 = jnp.bfloat16


def swap(value, axis, flip):
    count = lax.axis_size(axis)
    return lax.ppermute(value, axis, [(i, i ^ flip) for i in range(count)])


def after(value, *others):
    return lax.optimization_barrier((value, *others))[0]


def spread(part, axis, unit, index, count, dim, then=()):
    out = jnp.zeros(part.shape[:dim] + (count,) + part.shape[dim:], part.dtype)
    pieces = [part] + [after(swap(part, axis, unit * d), *then) for d in range(1, count)]
    for d, piece in enumerate(pieces):
        out = lax.dynamic_update_slice_in_dim(out, jnp.expand_dims(piece, dim), index ^ d, dim)
    return out, pieces[1:]


def places():
    core = lax.axis_index("seq") % 2
    return core, lax.axis_index("seq") // 2, lax.axis_index("shard")


def by_core(core, own, other):
    return jnp.where(core == 0, own, other), jnp.where(core == 0, other, own)


def split_pays():
    count, shards = lax.axis_size("seq"), lax.axis_size("shard")
    return count == 8 and shards == 4


def halves(weight, core):
    width = weight.shape[1] // 2
    return lax.dynamic_slice_in_dim(weight, core * width, width, 1)


def quarter_rows(block):
    quarters = lax.axis_size("seq") // 2
    rows = block.shape[0] // quarters
    return lax.dynamic_slice_in_dim(block, (lax.axis_index("seq") // 2) * rows, rows, 0)


def stack(part, axis, unit, then=()):
    count = lax.axis_size(axis) // unit
    others = [after(swap(part, axis, unit * d), *then) for d in range(1, count)]
    return [part] + others


def down_rows(quarter):
    return 72 * quarter + 8 * (quarter % 2)


def down_part(block, rows):
    quarter = lax.axis_index("seq") // 2
    padded = jnp.pad(block, ((0, 16), (0, 0)))
    part = lax.dynamic_slice_in_dim(padded, down_rows(quarter), 80, 0)
    return pack_down(part[None], rows)


def pack_down(blocks, rows):
    rest = blocks.shape[1] - rows
    second = jnp.pad(blocks[:, rows:], ((0, 0), (0, rows - rest), (0, 0)))
    columns = blocks.shape[2]
    return [blocks[:, :rows].reshape(-1, columns), second.reshape(-1, columns)]


def unpack_down(packed, blocks, rest):
    columns = packed.shape[1] // 2
    packed = packed.reshape(blocks, -1, 2 * columns)
    whole = jnp.concatenate([packed[:, :, :columns], packed[:, :rest, columns:]], axis=1)
    return whole.reshape(-1, columns)


def side_by_side(first, second):
    return jnp.concatenate([first, second], axis=1)


def total_of(pieces):
    total = pieces[0].astype(f32)
    for piece in pieces[1:]:
        total = total + piece.astype(f32)
    return total.astype(bf16)


def keep_half(own, got):
    shards, quarters = lax.axis_size("shard"), lax.axis_size("seq") // 2
    return total_of([own, got]).reshape(shards, quarters, -1, own.shape[1])


def sum_after(parts, *others):
    return total_of(parts[:1] + [after(part, *others) for part in parts[1:]])


def pieces(value, axis, unit, index, count, dim):
    def at(place):
        return lax.dynamic_index_in_dim(value, place, dim, keepdims=False)

    return [at(index)] + [swap(at(index ^ d), axis, unit * d) for d in range(1, count)]


def quarter_pieces(half):
    return pieces(half, "seq", 2, lax.axis_index("seq") // 2, lax.axis_size("seq") // 2, 1)


def shard_pieces(half):
    return pieces(half, "shard", 1, lax.axis_index("shard"), lax.axis_size("shard"), 0)


def owners_half(part, then=()):
    count = lax.axis_size("seq")
    part, _ = spread(part, "seq", 2, lax.axis_index("seq") // 2, count // 2, 0, then)
    return part.reshape(-1, part.shape[-1])


def reduce_whole(grad):
    owned = lax.psum_scatter(grad, "shard", scatter_dimension=0, tiled=True)
    return lax.psum(owned.astype(f32), "seq")


def gain_grad(weight, gradient, gain):
    low = weight.astype(bf16).astype(f32)
    return jnp.sum(low * gradient.astype(f32), axis=1) / gain.astype(bf16).astype(f32)


def to_right(value):
    axes = ("seq", "shard")
    ends = lax.axis_size(axes) - 1
    return lax.ppermute(value, axes, [(i, i + 1) for i in range(ends)])


def to_left(value):
    axes = ("seq", "shard")
    ends = lax.axis_size(axes) - 1
    return lax.ppermute(value, axes, [(i + 1, i) for i in range(ends)])


def normed(hidden):
    centered = hidden - jnp.mean(hidden, axis=-1, keepdims=True)
    inverse = lax.rsqrt(jnp.mean(centered * centered, axis=-1, keepdims=True) + norm_epsilon)
    return centered * inverse, inverse


def normed_back(grad, gain, unit, inverse):
    inner = grad * gain
    mean = jnp.mean(inner, axis=-1, keepdims=True)
    slope = jnp.mean(inner * unit, axis=-1, keepdims=True)
    return inverse * (inner - mean - unit * slope)


def dot(a, b):
    return jnp.dot(a, b, preferred_element_type=f32)


def dot_rows(a, b):
    return lax.dot_general(a, b, (((1,), (1,)), ((), ())), preferred_element_type=f32)


def dot_columns(a, b):
    return lax.dot_general(a, b, (((0,), (0,)), ((), ())), preferred_element_type=f32)


def turned(values):
    lane = lax.broadcasted_iota(jnp.int32, values.shape, 1)
    up = pltpu.roll(values, LANES - 32, 1)
    down = pltpu.roll(values, 32, 1)
    return jnp.where(lane % 64 < 32, up, down)


def rope(values, cos, sin):
    return values * cos + turned(values) * sin


def rope_back(values, cos, sin):
    return values * cos - turned(values) * sin


def mask_bias(meta_ref, block):
    first = block * ROWS
    shape = (SPAN, LANES)
    key = lax.broadcasted_iota(jnp.int32, shape, 0) + (first - HALF)
    query = lax.broadcasted_iota(jnp.int32, shape, 1) % ROWS + first
    start, low, high = meta_ref[0], meta_ref[1], meta_ref[2]
    apart = jnp.abs(query - key) > HALF
    other = (query >= start) != (key >= start)
    outside = (key < low) | (key >= high)
    return jnp.where(apart | other | outside, masked_score, 0.0).astype(f32)


def stacked(values):
    lane = lax.broadcasted_iota(jnp.int32, values.shape, 1)
    zero = jnp.zeros_like(values)
    return jnp.concatenate(
        [jnp.where(lane < 64, values, zero), jnp.where(lane < 64, zero, values)], axis=0
    )


def unstacked(even, odd):
    lane = lax.broadcasted_iota(jnp.int32, (64, LANES), 1)
    top = jnp.where(lane < ROWS, even[:64], pltpu.roll(odd[:64], ROWS, 1))
    bottom = jnp.where(lane < ROWS, pltpu.roll(even[64:], ROWS, 1), odd[64:])
    return jnp.concatenate([top, bottom], axis=0)


def window(block):
    return slice(block * ROWS, block * ROWS + SPAN)


def turned_window(kt, kt_odd, block):
    at = (block // 2) * PAIR
    return (kt_odd if block % 2 else kt)[:, at : at + SPAN]


def assemble(place_ref, shards, quarters, copy):
    for c in (0, 1):

        @pl.when(place_ref[0] == c)
        def _(c=c):
            for side in (0, 1):
                for dq in range(quarters):
                    for dz in range(shards):
                        copy(
                            side,
                            c ^ side,
                            dq * shards + dz,
                            jnp.bitwise_xor(place_ref[1], dq),
                            jnp.bitwise_xor(place_ref[2], dz),
                        )


def project_kernel(x_ref, gain_ref, w_ref, cos_ref, sin_ref, h_ref, q_ref, k_ref, v_ref):
    unit, _ = normed(x_ref[...].astype(f32))
    low = (unit * gain_ref[0:1, :]).astype(bf16)
    h_ref[...] = low
    width = low.shape[1]
    cos, sin = cos_ref[...], sin_ref[...]
    for ref, at, scale in ((q_ref, 0, 0.125), (k_ref, width, None)):
        out = dot(low, w_ref[:, at : at + width])
        for j in range(0, width, LANES):
            value = rope(out[:, j : j + LANES], cos, sin)
            if scale is not None:
                value = value * scale
            ref[:, j : j + LANES] = value.astype(bf16)
    v_ref[...] = dot(low, w_ref[:, 2 * width :]).astype(bf16)


def project_edges_kernel(
    split, place_ref, x_ref, gain_ref, cos_ref, sin_ref, *refs
):
    *parts, head_ref, tail_ref, w_ref = refs
    if split:
        shards, quarters = split
        rows = parts[0].shape[0] // (shards * quarters)
        half = parts[0].shape[1]

        def copy(side, column, part, quarter, shard):
            at = pl.multiple_of((shard * quarters + quarter) * rows, 16)
            w_ref[pl.ds(at, rows), column * half : (column + 1) * half] = parts[side][
                part * rows : (part + 1) * rows, :
            ]

        assemble(place_ref, shards, quarters, copy)
    else:
        w_ref[...] = parts[0][...]
    unit, _ = normed(x_ref[...].astype(f32))
    low = (unit * gain_ref[0:1, :]).astype(bf16)
    width = low.shape[1]
    cos, sin = cos_ref[...], sin_ref[...]
    keys = dot(low, w_ref[:, width : 2 * width])
    for j in range(0, width, LANES):
        value = rope(keys[:, j : j + LANES], cos, sin).astype(bf16)
        head_ref[:, j : j + LANES] = value[:HALF]
        tail_ref[:, j : j + LANES] = value[HALF:]
    values = dot(low, w_ref[:, 2 * width :]).astype(bf16)
    head_ref[:, width:] = values[:HALF]
    tail_ref[:, width:] = values[HALF:]


def fill(dst, left, middle, right):
    rows = middle.shape[0]
    dst[0:HALF, :] = left[...]
    dst[HALF : HALF + rows, :] = middle[...]
    dst[HALF + rows :, :] = right[...]


def flip(dst, src, start, stop, shift):
    for at in range(start, stop, LANES):
        end = min(at + LANES, stop)
        dst[:, at - shift : end - shift] = src[at:end, :].T


def attend_kernel(
    meta_ref, q_ref, k_ref, v_ref, kl_ref, vl_ref, kr_ref, vr_ref, *refs
):
    o_ref, lse_ref, kx, vx, bias, vt, vt_odd = refs[-7:]
    blocks = q_ref.shape[0] // ROWS

    @pl.when(pl.program_id(0) == 0)
    def _():
        for n in range(blocks):
            bias[n] = mask_bias(meta_ref, n)

    fill(kx, kl_ref, k_ref, kr_ref)
    fill(vx, vl_ref, v_ref, vr_ref)
    flip(vt, vx, 0, vx.shape[0], 0)
    flip(vt_odd, vx, ROWS, vx.shape[0], ROWS)
    outs = []
    for n in range(blocks):
        queries = stacked(q_ref[n * ROWS : (n + 1) * ROWS, :])
        scores = dot_rows(kx[window(n), :], queries) + bias[n]
        top = jnp.max(scores, axis=0, keepdims=True)
        weights = jnp.exp(scores - top)
        total = jnp.sum(weights, axis=0, keepdims=True)
        out = dot(turned_window(vt, vt_odd, n), weights.astype(bf16))
        outs.append(out * (1.0 / total))
        lse_ref[0, n : n + 1, :] = top + jnp.log(total)
        if n % 2:
            at = (n // 2) * PAIR
            o_ref[:, at : at + PAIR] = unstacked(*outs[-2:]).astype(bf16)


def back_blocks(
    halves, dq_at, q_ref, do_ref, kx, vx, bias, kt, kt_odd, lse_ref, cos_ref, sin_ref, dq_ref, dkx, dvx
):
    for m in halves:
        outs = []
        for n in (2 * m, 2 * m + 1):
            own = slice(n * ROWS, (n + 1) * ROWS)
            queries = stacked(q_ref[own, :])
            grads = stacked(do_ref[own, :])
            scores = dot_rows(kx[window(n), :], queries) + bias[n]
            probs = jnp.exp(scores - lse_ref[0, n : n + 1, :])
            grad_probs = dot_rows(vx[window(n), :], grads)
            inner = jnp.sum(probs * grad_probs, axis=0, keepdims=True)
            grad_scores = (probs * (grad_probs - inner)).astype(bf16)
            dvx[window(n), :] += dot(probs.astype(bf16), grads)
            dkx[window(n), :] += dot(grad_scores, queries)
            outs.append(dot(turned_window(kt, kt_odd, n), grad_scores))
        own = slice(m * PAIR, (m + 1) * PAIR)
        grad_query = unstacked(*outs).T * 0.125
        at = dq_at(m) * PAIR
        dq_ref[at : at + PAIR, :] = rope_back(
            grad_query, cos_ref[own, :], sin_ref[own, :]
        ).astype(bf16)


def attend_back_edges_kernel(
    meta_ref, q_ref, k_ref, v_ref, do_ref, kl_ref, vl_ref, kr_ref, vr_ref, lse_ref, cos_ref, sin_ref,
    dq_ref, wk_ref, wv_ref, head_ref, tail_ref, ek_ref, ev_ref,
    kx, vx, bias, kt, kt_odd, dkx, dvx,
):
    rows = q_ref.shape[0]
    blocks = rows // PAIR
    span = PAIR + 2 * HALF
    spans = (slice(0, span), slice(rows - PAIR, rows + 2 * HALF))

    @pl.when(pl.program_id(0) == 0)
    def _():
        for n in (0, 1, 2 * blocks - 2, 2 * blocks - 1):
            bias[n] = mask_bias(meta_ref, n)

    fill(kx, kl_ref, k_ref, kr_ref)
    fill(vx, vl_ref, v_ref, vr_ref)
    for own in spans:
        flip(kt, kx, own.start, own.stop, 0)
        flip(kt_odd, kx, own.start + ROWS, own.stop, ROWS)
        for acc in (dkx, dvx):
            acc[own, :] = jnp.zeros((span, LANES), f32)
    back_blocks(
        (0, blocks - 1), lambda n: min(n, 1),
        q_ref, do_ref, kx, vx, bias, kt, kt_odd, lse_ref, cos_ref, sin_ref, dq_ref, dkx, dvx,
    )
    for ref, acc in ((wk_ref, dkx), (wv_ref, dvx)):
        ref[:span, :] = acc[spans[0], :]
        ref[span:, :] = acc[spans[1], :]
    for at, acc, ref in ((0, dkx, ek_ref), (1, dvx, ev_ref)):
        head_ref[at] = acc[0:HALF, :].astype(bf16)
        tail_ref[at] = acc[HALF + rows :, :].astype(bf16)
        ref[0:HALF, :] = acc[HALF : 2 * HALF, :]
        ref[HALF:, :] = acc[rows : rows + HALF, :]


def attend_back_kernel(
    meta_ref, q_ref, k_ref, v_ref, do_ref, kl_ref, vl_ref, kr_ref, vr_ref, lse_ref, cos_ref, sin_ref,
    eq_ref, wk_ref, wv_ref,
    dq_ref, dk_ref, dv_ref,
    kx, vx, bias, kt, kt_odd, dkx, dvx,
):
    rows = q_ref.shape[0]
    blocks = rows // PAIR
    span = PAIR + 2 * HALF

    @pl.when(pl.program_id(0) == 0)
    def _():
        for n in range(2, 2 * blocks - 2):
            bias[n] = mask_bias(meta_ref, n)

    fill(kx, kl_ref, k_ref, kr_ref)
    fill(vx, vl_ref, v_ref, vr_ref)
    flip(kt, kx, 0, kx.shape[0], 0)
    flip(kt_odd, kx, ROWS, kx.shape[0], ROWS)
    last = slice(rows - PAIR, rows + 2 * HALF)
    for acc, ref in ((dkx, wk_ref), (dvx, wv_ref)):
        acc[:span, :] = ref[:span, :]
        acc[span : last.start, :] = jnp.zeros((last.start - span, LANES), f32)
        acc[last, :] = ref[span:, :]
    dq_ref[:PAIR, :] = eq_ref[:PAIR, :]
    dq_ref[rows - PAIR :, :] = eq_ref[PAIR:, :]
    back_blocks(
        range(1, blocks - 1), lambda n: n,
        q_ref, do_ref, kx, vx, bias, kt, kt_odd, lse_ref, cos_ref, sin_ref, dq_ref, dkx, dvx,
    )
    middle = slice(HALF, HALF + rows)
    dk_ref[...] = rope_back(dkx[middle, :], cos_ref[...], sin_ref[...]).astype(bf16)
    dv_ref[...] = dvx[middle, :].astype(bf16)


def pack_grads(ref, c, slots, acc_d, acc_m, acc_a):
    wide, narrow = acc_m.shape[1] // 2, acc_a.shape[1] // 2
    rows, down_rows = acc_m.shape[0] // slots, acc_d.shape[0] // slots
    ref[:, :wide] = acc_m[:, c * wide : (c + 1) * wide].astype(bf16)
    ref[:, wide : wide + narrow] = acc_a[:, c * narrow : (c + 1) * narrow].astype(bf16)
    fill_rows = jnp.zeros((2 * rows - down_rows, narrow), f32)
    for n in range(slots):
        own = slice(n * rows, (n + 1) * rows)
        block = acc_d[n * down_rows : (n + 1) * down_rows, c * narrow : (c + 1) * narrow]
        ref[own, wide + narrow : wide + 2 * narrow] = block[:rows].astype(bf16)
        rest = jnp.concatenate([block[rows:], fill_rows], axis=0)
        ref[own, wide + 2 * narrow :] = rest.astype(bf16)


def gather_middle(split, place_ref, step, parts, wa_ref, wm_ref, wd_ref):
    shards, quarters = split
    rows = parts[0].shape[0] // (shards * quarters)
    wide, narrow = wm_ref.shape[1] // 2, wa_ref.shape[1] // 2
    shard_rows = wd_ref.shape[0] // shards

    def copy(side, column, part, quarter, shard):
        own = slice(part * rows, (part + 1) * rows)
        ref = parts[side]
        lanes = slice(column * narrow, (column + 1) * narrow)
        at = pl.multiple_of((shard * quarters + quarter) * rows, 16)
        wm_ref[pl.ds(at, rows), column * wide : (column + 1) * wide] = ref[own, :wide]
        wa_ref[pl.ds(at, rows), lanes] = ref[own, wide : wide + narrow]
        at = shard * shard_rows + down_rows(quarter)
        first, second = wide + narrow, wide + 2 * narrow
        wd_ref[pl.ds(pl.multiple_of(at, 16), rows), lanes] = ref[own, first:second]
        rest = ref[own, second:]
        wd_ref[pl.ds(pl.multiple_of(at + rows, 16), 16), lanes] = rest[:16]

        @pl.when(quarter % 2 == 0)
        def _():
            wd_ref[pl.ds(pl.multiple_of(at + rows + 16, 16), 16), lanes] = rest[16:32]

    @pl.when(step == 0)
    def _():
        assemble(place_ref, shards, quarters, copy)


def middle_kernel(
    split, place_ref, x_ref, o_ref, ct_ref, gain_ref, *refs
):
    *refs, acc_d, acc_m, acc_a = refs
    step = pl.program_id(0)
    if split:
        own_part, other_part, out_ref, dmid_ref, do_ref, own_ref, other_ref, wa_ref, wm_ref, wd_ref = refs
        gather_middle(split, place_ref, step, (own_part, other_part), wa_ref, wm_ref, wd_ref)
    else:
        wa_ref, wm_ref, wd_ref, out_ref, dmid_ref, do_ref, *grad_refs = refs

    @pl.when(step == 0)
    def _():
        acc_d[...] = jnp.zeros_like(acc_d)
        acc_m[...] = jnp.zeros_like(acc_m)
        acc_a[...] = jnp.zeros_like(acc_a)

    gain = gain_ref[1:2, :]
    hidden = wd_ref.shape[0]
    chunk = hidden // 3
    ct = ct_ref[...]
    mid = x_ref[...].astype(f32) + dot_columns(o_ref[...], wa_ref[...])
    unit, inverse = normed(mid)
    low = (unit * gain).astype(bf16)
    low_t = low.T
    out = mid
    dh = jnp.zeros_like(mid)
    for at in range(0, hidden, chunk):
        first, second = slice(at, at + chunk), slice(hidden + at, hidden + at + chunk)
        a1 = dot(low, wm_ref[:, first])
        a2 = dot(low, wm_ref[:, second])
        du = dot_rows(ct, wd_ref[first, :])
        phi = 0.5 * (1.0 + lax.erf(a1 * (1.0 / math.sqrt(2.0))))
        gate = a1 * phi
        u = (gate * a2).astype(bf16)
        slope = phi + a1 * (jnp.exp(-0.5 * a1 * a1) * (1.0 / math.sqrt(2.0 * math.pi)))
        da1 = (du * a2 * slope).astype(bf16)
        da2 = (du * gate).astype(bf16)
        out = out + dot(u, wd_ref[first, :])
        dh = dh + dot_rows(da1, wm_ref[:, first]) + dot_rows(da2, wm_ref[:, second])
        acc_d[first, :] += dot_columns(u, ct)
        acc_m[:, first] += dot(low_t, da1)
        acc_m[:, second] += dot(low_t, da2)
    out_ref[...] = out.astype(bf16)
    dmid = ct.astype(f32) + normed_back(dh, gain, unit, inverse)
    dmr = dmid.astype(bf16)
    dmid_ref[...] = dmr
    acc_a[...] += dot(o_ref[...], dmr)
    do_ref[...] = dot_rows(dmr, wa_ref[...]).astype(bf16)

    last = step == pl.num_programs(0) - 1
    if not split:

        @pl.when(last)
        def _():
            for ref, acc in zip(grad_refs, (acc_d, acc_m, acc_a)):
                ref[...] = acc[...].astype(bf16)

    else:
        slots = split[0] * split[1]
        for c in (0, 1):

            @pl.when(last & (place_ref[0] == c))
            def _(c=c):
                pack_grads(own_ref, c, slots, acc_d, acc_m, acc_a)
                pack_grads(other_ref, 1 - c, slots, acc_d, acc_m, acc_a)


def patched(step, steps, rows, value_ref, edge_ref):
    value = value_ref[...]
    edge = edge_ref[...]
    head = jnp.concatenate([edge[:HALF], value[HALF:]], axis=0)
    value = jnp.where(step == 0, head, value)
    tail = jnp.concatenate([value[: rows - HALF], edge[HALF:]], axis=0)
    return jnp.where(step == steps - 1, tail, value)


def qkv_grad_kernel(
    split, place_ref,
    h_ref, dq_ref, dk_ref, dv_ref, rk_ref, rv_ref, left_ref, right_ref, cos_ref, sin_ref,
    ek_ref, ev_ref, *refs,
):
    *grad_refs, acc = refs
    step, steps = pl.program_id(0), pl.num_programs(0)
    rows, width = h_ref.shape

    @pl.when(step == 0)
    def _():
        for at, side in ((0, left_ref), (HALF, right_ref)):
            own = slice(at, at + HALF)
            cos, sin = cos_ref[own, :], sin_ref[own, :]
            for j in range(0, width, LANES):
                lanes = slice(j, j + LANES)
                total = rk_ref[own, lanes] + side[0, :, lanes].astype(f32)
                ek_ref[own, lanes] = rope_back(total, cos, sin).astype(bf16)
            ev_ref[own, :] = (rv_ref[own, :] + side[1].astype(f32)).astype(bf16)

    @pl.when(step == 0)
    def _():
        acc[...] = jnp.zeros_like(acc)

    low = h_ref[...]
    acc[:, :width] += dot_columns(low, dq_ref[...])
    acc[:, width : 2 * width] += dot_columns(low, patched(step, steps, rows, dk_ref, ek_ref))
    acc[:, 2 * width :] += dot_columns(low, patched(step, steps, rows, dv_ref, ev_ref))

    last = step == steps - 1
    if not split:

        @pl.when(last)
        def _():
            grad_refs[0][...] = acc[...].astype(bf16)

    else:
        half = acc.shape[1] // 2
        for c in (0, 1):

            @pl.when(last & (place_ref[0] == c))
            def _(c=c):
                for ref, side in zip(grad_refs, (c, 1 - c)):
                    ref[...] = acc[:, side * half : (side + 1) * half].astype(bf16)


def input_kernel(x_ref, gain_ref, w_ref, dmid_ref, dq_ref, dk_ref, dv_ref, ek_ref, ev_ref, dx_ref):
    step, steps = pl.program_id(0), pl.num_programs(0)
    rows, width = x_ref.shape

    dh = dot_rows(dq_ref[...], w_ref[:, :width])
    dh = dh + dot_rows(patched(step, steps, rows, dk_ref, ek_ref), w_ref[:, width : 2 * width])
    dh = dh + dot_rows(patched(step, steps, rows, dv_ref, ev_ref), w_ref[:, 2 * width :])
    unit, inverse = normed(x_ref[...].astype(f32))
    dx = dmid_ref[...].astype(f32) + normed_back(dh, gain_ref[0:1, :], unit, inverse)
    dx_ref[...] = dx.astype(bf16)


def shaped(shape, dtype):
    return jax.ShapeDtypeStruct(shape, dtype)


def tiles(rows, columns):
    return pl.BlockSpec((rows, columns), lambda i: (i, 0))


def pairs(rows, offset=0):
    return pl.BlockSpec((rows, LANES), lambda i: (0, i + offset))


def kept(*shape):
    return pl.BlockSpec(shape, lambda i: (0,) * len(shape), pipeline_mode=pl.Buffered(1))


def held(*shape):
    return pl.BlockSpec(shape, lambda i: (0,) * len(shape))


def call(
    kernel, grid, in_specs, out_specs, out_shape, scratch, flops, moved, aliases=None
):
    return pl.pallas_call(
        kernel,
        grid=(grid,),
        in_specs=in_specs,
        out_specs=out_specs,
        out_shape=out_shape,
        scratch_shapes=scratch,
        input_output_aliases=aliases or {},
        compiler_params=pltpu.CompilerParams(
            vmem_limit_bytes=vmem_bytes, dimension_semantics=("arbitrary",)
        ),
        cost_estimate=pl.CostEstimate(
            flops=flops // 64, bytes_accessed=moved // 64, transcendentals=0
        ),
    )


def project(x, gains, weight, cos, sin):
    rows, width = x.shape
    tile = min(TILE, rows)
    return call(
        project_kernel,
        rows // tile,
        [tiles(tile, width), held(2, width), kept(*weight.shape), tiles(tile, LANES), tiles(tile, LANES)],
        [tiles(tile, width)] * 4,
        [shaped((rows, width), bf16)] * 4,
        [],
        2 * rows * width * 3 * width,
        rows * width * 10 + weight.size * 2,
    )(x, gains, weight, cos, sin)


def project_edges(split, place, x, gains, cos, sin, *parts):
    rows, width = x.shape
    return call(
        functools.partial(project_edges_kernel, split),
        1,
        [pl.BlockSpec(memory_space=pltpu.SMEM), held(rows, width), held(2, width)]
        + [held(rows, LANES)] * 2
        + [held(*part.shape) for part in parts],
        [held(HALF, 2 * width)] * 2 + [held(width, 3 * width)],
        [shaped((HALF, 2 * width), bf16)] * 2 + [shaped((width, 3 * width), bf16)],
        [],
        4 * rows * width * width,
        rows * width * 6 + width * width * 12,
    )(place, x, gains, cos, sin, *parts)


def attend_scratch(rows):
    extended = rows + 2 * HALF
    return [
        pltpu.VMEM((extended, LANES), bf16),
        pltpu.VMEM((extended, LANES), bf16),
        pltpu.VMEM((rows // ROWS, SPAN, LANES), f32),
        pltpu.VMEM((LANES, extended), bf16),
        pltpu.VMEM((LANES, extended - ROWS), bf16),
    ]


def attend(meta, q, k, v, left, right, first, count, before=()):
    rows, width = q.shape
    steps = width // LANES

    def columns(height, offset=0):
        return pairs(height, first + offset)

    return call(
        attend_kernel,
        count,
        [pl.BlockSpec(memory_space=pltpu.SMEM)]
        + [columns(rows)] * 3
        + [columns(HALF), columns(HALF, steps)] * 2
        + [pl.BlockSpec(memory_space=pl.ANY)] * len(before),
        [
            pl.BlockSpec((LANES, rows), lambda i: (i + first, 0)),
            pl.BlockSpec((1, rows // ROWS, LANES), lambda i: (i + first, 0, 0)),
        ],
        [shaped((width, rows), bf16), shaped((steps, rows // ROWS, LANES), f32)],
        attend_scratch(rows),
        8 * rows * width * 256,
        rows * width * 8,
        {8 + at: at for at in range(len(before))},
    )(meta, q, k, v, left, left, right, right, *before)


def back_specs(rows, steps):
    return (
        [pl.BlockSpec(memory_space=pltpu.SMEM)]
        + [pairs(rows)] * 4
        + [pairs(HALF), pairs(HALF, steps)] * 2
        + [pl.BlockSpec((1, rows // ROWS, LANES), lambda i: (i, 0, 0)), held(rows, LANES), held(rows, LANES)]
    )


def back_scratch(rows):
    extended = rows + 2 * HALF
    return attend_scratch(rows) + [pltpu.VMEM((extended, LANES), f32)] * 2


def attend_back_edges(meta, q, k, v, do, left, right, lse, cos, sin):
    rows, width = q.shape
    steps = width // LANES
    span = 2 * (PAIR + 2 * HALF)
    return call(
        attend_back_edges_kernel,
        steps,
        back_specs(rows, steps),
        [pairs(2 * PAIR)]
        + [pairs(span)] * 2
        + [pl.BlockSpec((2, HALF, LANES), lambda i: (0, 0, i))] * 2
        + [pairs(2 * HALF)] * 2,
        [shaped((2 * PAIR, width), bf16)]
        + [shaped((span, width), f32)] * 2
        + [shaped((2, HALF, width), bf16)] * 2
        + [shaped((2 * HALF, width), f32)] * 2,
        back_scratch(rows),
        20 * 2 * PAIR * width * 256,
        rows * width * 10,
    )(meta, q, k, v, do, left, left, right, right, lse, cos, sin)


def attend_back(meta, q, k, v, do, left, right, lse, cos, sin, edges):
    rows, width = q.shape
    steps = width // LANES
    span = 2 * (PAIR + 2 * HALF)
    return call(
        attend_back_kernel,
        steps,
        back_specs(rows, steps) + [pairs(2 * PAIR)] + [pairs(span)] * 2,
        [pairs(rows)] * 3,
        [shaped((rows, width), bf16)] * 3,
        back_scratch(rows),
        20 * rows * width * 256,
        rows * width * 14,
    )(meta, q, k, v, do, left, left, right, right, lse, cos, sin, *edges)


def middle(split, place, x, o, ct, gains, shapes, *weights):
    rows, width = x.shape
    tile = WIDE_TILE if rows % WIDE_TILE == 0 else rows
    wa, wm, wd = shapes
    if split:
        grads = [(width, wm[1] // 2 + 3 * (width // 2))] * 2
    else:
        grads = [wd, wm, wa]
    return call(
        functools.partial(middle_kernel, split),
        rows // tile,
        [
            pl.BlockSpec(memory_space=pltpu.SMEM),
            tiles(tile, width),
            pl.BlockSpec((width, tile), lambda i: (0, i)),
            tiles(tile, width),
            held(2, width),
        ]
        + [kept(*w.shape) for w in weights],
        [tiles(tile, width)] * 3 + [kept(*shape) for shape in grads],
        [shaped((rows, width), bf16)] * 3 + [shaped(shape, bf16) for shape in grads],
        ([pltpu.VMEM(w, bf16) for w in shapes] if split else [])
        + [pltpu.VMEM(wd, f32), pltpu.VMEM(wm, f32), pltpu.VMEM(wa, f32)],
        6 * rows * width * width * 5,
        rows * width * 14 + 20 * width * width,
    )(place, x, o, ct, gains, *weights)


def qkv_gradient(split, place, h, dq, dk, dv, ek, ev, left, right, cos, sin):
    rows, width = h.shape
    tile = WIDE_TILE if rows % WIDE_TILE == 0 else rows
    grads = [(width, 3 * width // 2)] * 2 if split else [(width, 3 * width)]
    return call(
        functools.partial(qkv_grad_kernel, split),
        rows // tile,
        [pl.BlockSpec(memory_space=pltpu.SMEM)]
        + [tiles(tile, width)] * 4
        + [held(2 * HALF, width)] * 2
        + [held(2, HALF, width)] * 2
        + [held(2 * HALF, LANES)] * 2,
        [held(2 * HALF, width)] * 2 + [held(*shape) for shape in grads],
        [shaped((2 * HALF, width), bf16)] * 2 + [shaped(shape, bf16) for shape in grads],
        [pltpu.VMEM((width, 3 * width), f32)],
        6 * rows * width * width,
        rows * width * 8 + 6 * width * width,
    )(place, h, dq, dk, dv, ek, ev, left, right, cos, sin)


def input_gradient(x, gains, weight, dmid, dq, dk, dv, ek, ev):
    rows, width = x.shape
    tile = min(TILE, rows)
    return call(
        input_kernel,
        rows // tile,
        [tiles(tile, width), held(2, width), kept(*weight.shape)]
        + [tiles(tile, width)] * 4
        + [held(2 * HALF, width)] * 2,
        tiles(tile, width),
        shaped((rows, width), bf16),
        [],
        6 * rows * width * width,
        rows * width * 14 + 6 * width * width,
    )(x, gains, weight, dmid, dq, dk, dv, ek, ev)


def rope_tables(positions, head_size):
    half_size = head_size // 2
    exponent = jnp.arange(half_size, dtype=f32) * (2.0 / head_size)
    inverse = rope_theta ** (-exponent)
    inverse = jnp.tile(inverse, LANES // half_size)
    angles = positions.astype(f32)[:, None] * inverse[None, :]
    sign = jnp.where(jnp.arange(LANES) % head_size < half_size, -1.0, 1.0).astype(f32)
    return jnp.cos(angles), jnp.sin(angles) * sign


def adam_update(master, first_moment, second_moment, gradient, step_rate):
    gradient = gradient.astype(f32)
    new_first = beta_first * first_moment + (1.0 - beta_first) * gradient
    new_second = beta_second * second_moment + (1.0 - beta_second) * gradient * gradient
    first_hat = new_first / (1.0 - beta_first**ADAM_STEP)
    second_hat = new_second / (1.0 - beta_second**ADAM_STEP)
    new_master = master - step_rate * (
        decay_rate * master + first_hat / (jnp.sqrt(second_hat) + adam_epsilon)
    )
    return (new_first, new_second, new_master)


def edge_rows(value):
    return value[:HALF], value[value.shape[0] - HALF :]


def per_device(
    tokens,
    positions,
    cotangent,
    qkv_weight,
    attn_weight,
    mlp_weight,
    down_weight,
    norm_gains,
    qkv_first,
    qkv_second,
    attn_first,
    attn_second,
    mlp_first,
    mlp_second,
    down_first,
    down_second,
    gains_first,
    gains_second,
):
    rows, width = tokens.shape
    device = lax.axis_index(("seq", "shard"))
    last_device = lax.axis_size(("seq", "shard")) - 1
    cos, sin = rope_tables(positions, width // HEADS)
    start = jnp.max(jnp.where(positions == 0, jnp.arange(rows, dtype=jnp.int32), 0))
    low = jnp.where(device > 0, -HALF, 0)
    high = jnp.where(device < last_device, rows + HALF, rows)
    meta = jnp.stack([start, low, high]).astype(jnp.int32)
    shards = lax.axis_size("shard")
    quarters = lax.axis_size("seq") // 2
    core = lax.axis_index("seq") % 2
    split = (shards, quarters) if split_pays() else None
    place = jnp.stack([core, lax.axis_index("seq") // 2, lax.axis_index("shard")])
    place = place.astype(jnp.int32)
    half = qkv_weight.shape[1] // 2
    slot = qkv_weight.shape[0] // quarters
    rest = down_weight.shape[0] // quarters - slot
    wide = mlp_weight.shape[1] // 2
    down_at = wide + attn_weight.shape[1] // 2
    lows = [w.astype(bf16) for w in (qkv_weight, attn_weight, mlp_weight, down_weight)]
    if split:
        qkv_low, attn_low, mlp_low, down_low = lows
        part = quarter_rows(halves(qkv_low, core))
        gain_rows = jnp.pad(norm_gains.astype(bf16), ((0, 6), (0, half - norm_gains.shape[1])))
        qkv_stack = stack(jnp.concatenate([part, gain_rows], axis=0), "shard", 1)
        gains = jnp.zeros((shards, 2, norm_gains.shape[1]), bf16)
        for d, piece in enumerate(qkv_stack):
            piece = piece[None, slot : slot + 2, : norm_gains.shape[1]]
            gains = lax.dynamic_update_slice_in_dim(gains, piece, lax.axis_index("shard") ^ d, 0)
        gains = gains.astype(f32).transpose(1, 0, 2).reshape(2, -1)
        rest_part = jnp.concatenate(
            [quarter_rows(halves(w, core)) for w in (mlp_low, attn_low)]
            + down_part(halves(down_low, core), slot),
            axis=1,
        )
        rest_part = jnp.concatenate(
            stack(after(rest_part, qkv_stack[1]), "shard", 1), axis=0
        )
        qkv_part = jnp.concatenate([piece[:slot] for piece in qkv_stack], axis=0)
        qkv_part = jnp.concatenate(stack(qkv_part, "seq", 2), axis=0)
        qkv_part = after(qkv_part, rest_part)
        rest_part = after(rest_part, qkv_part)
        qkv_parts = qkv_part, swap(qkv_part, "seq", 1)
    else:
        full_qkv, full_attn, full_mlp, full_down = (
            lax.all_gather(w, "shard", axis=0, tiled=True) for w in lows
        )
        gains = lax.all_gather(norm_gains.astype(bf16), "shard", axis=1, tiled=True).astype(f32)
        qkv_parts = (full_qkv,)
    edge_x, edge_cos, edge_sin = (
        jnp.concatenate(edge_rows(value), axis=0) for value in (tokens, cos, sin)
    )
    kv_head, kv_tail, full_qkv = project_edges(
        split, place, edge_x, gains, edge_cos, edge_sin, *qkv_parts
    )
    left = to_right(kv_tail)
    right = to_left(kv_head)
    h, q, k, v = project(after(tokens, kv_head), gains, full_qkv, cos, sin)
    left = after(left, k)
    right = after(right, k)
    pair_count = width // LANES
    before = attend(meta, q, k, v, left, right, 0, pair_count // 2)
    if split:
        rest_part = jnp.concatenate(stack(rest_part, "seq", 2, (before[0],)), axis=0)
        rest_weights = rest_part, swap(rest_part, "seq", 1)
        q = after(q, rest_part)
    else:
        rest_weights = full_attn, full_mlp, full_down
    o, lse = attend(
        meta, q, k, v, left, right, pair_count // 2, pair_count - pair_count // 2, before
    )
    shapes = (
        (width, attn_weight.shape[1]),
        (width, mlp_weight.shape[1]),
        (shards * down_weight.shape[0], width),
    )
    layer_output, dmid, do, *rest_grads = middle(
        split, place, tokens, o, cotangent, gains, shapes, *rest_weights
    )
    if split:
        rest_own, rest_other = rest_grads
        rest_got = swap(rest_other, "seq", 1)
    back_args = (meta, q, k, v, do, left, right, lse, cos, sin)
    *edges, halo_head, halo_tail, raw_k, raw_v = attend_back_edges(*back_args)
    from_right = to_left(halo_head)
    from_left = to_right(halo_tail)
    if split:
        rest_half = keep_half(rest_own, after(rest_got, halo_head))
        do = after(do, rest_half)
        back_args = (meta, q, k, v, do, left, right, lse, cos, sin)
        rest_pieces = quarter_pieces(rest_half)
    dq, dk, dv = attend_back(*back_args, edges)
    edge_k, edge_v, *qkv_grads = qkv_gradient(
        split, place, h, dq, dk, dv, raw_k, raw_v, after(from_left, dq), after(from_right, dq), edge_cos, edge_sin
    )
    if split:
        qkv_own, qkv_other = qkv_grads
        rest_part = sum_after(rest_pieces, qkv_own)
        qkv_got = swap(after(qkv_other, rest_part), "seq", 1)
        qkv_half = keep_half(qkv_own, qkv_got)
        dq = after(dq, qkv_half)
        qkv_pieces = quarter_pieces(qkv_half)
        rest_pieces = shard_pieces(rest_part)
    input_grad = input_gradient(tokens, gains, full_qkv, dmid, dq, dk, dv, edge_k, edge_v)
    if split:
        qkv_part = sum_after(qkv_pieces, input_grad)
        rest_part = sum_after(rest_pieces, qkv_part)
        qkv_part = sum_after(shard_pieces(qkv_part), rest_part)
        rest_half = owners_half(rest_part, (qkv_part,))
        rest_got = swap(rest_half, "seq", 1)
        qkv_half = owners_half(qkv_part, (rest_half,))
        qkv_got = swap(qkv_half, "seq", 1)
        first, second = by_core(core, rest_half, after(rest_got, qkv_half))
        mlp_total = side_by_side(first[:, :wide], second[:, :wide])
        attn_total = side_by_side(first[:, wide:down_at], second[:, wide:down_at])
        down_total = side_by_side(
            *(unpack_down(x[:, down_at:], quarters, rest) for x in (first, second))
        )
    else:
        down_total, mlp_total, attn_total, qkv_total = (
            reduce_whole(g) for g in (*rest_grads, *qkv_grads)
        )
    attn_new = adam_update(attn_weight, attn_first, attn_second, attn_total, rate_matrix)
    mlp_new = adam_update(mlp_weight, mlp_first, mlp_second, mlp_total, rate_matrix)
    down_new = adam_update(down_weight, down_first, down_second, down_total, rate_matrix)
    if split:
        qkv_got = after(qkv_got, attn_new[0], mlp_new[0], down_new[0])
        qkv_total = side_by_side(*by_core(core, qkv_half, qkv_got))
    qkv_new = adam_update(qkv_weight, qkv_first, qkv_second, qkv_total, rate_matrix)
    gains_total = jnp.stack(
        [
            gain_grad(qkv_weight, qkv_total, norm_gains[0]),
            gain_grad(mlp_weight, mlp_total, norm_gains[1]),
        ]
    )
    gains_new = adam_update(norm_gains, gains_first, gains_second, gains_total, rate_gains)
    return (layer_output, input_grad, *qkv_new, *attn_new, *mlp_new, *down_new, *gains_new)


def solution(mesh):
    tokens, rows, columns = P(("seq", "shard"), None), P("shard", None), P(None, "shard")
    matrices = (rows,) * 4
    return jax.shard_map(
        per_device,
        mesh=mesh,
        in_specs=(tokens, P(("seq", "shard")), tokens, *matrices, columns)
        + (rows,) * 8
        + (columns,) * 2,
        out_specs=(tokens, tokens) + (rows,) * 12 + (columns,) * 3,
        check_vma=False,
    )
```

profile of v0, /device:TPU:0, one launch (start us, length us, event | category | flops | bytes accessed | tf_op | source)
XLA Modules:
  0.0 329.5 jit_solution(3121819619418199919)
XLA Ops:
  0.7 2.6 convert_element_type.150
  5.7 3.0 collective-permute-start
  8.7 2.6 collective-permute-start.1
  17.5 3.0 fusion.14
  22.5 3.5 %collective-permute-start.7 = (bf16[48,2304]{1,0:T(8,128)(2,1)S(1)}, bf16[48,2304]{1,0:T(8,128)(2,1)S(1)}, u32[]{:S(2)}, u32[]{:S(2)}) collective-permute-start(bf16[48,2304]{1,0:T(8,128)(2,1)S(1)} %pad_maximum_fusion.6), channel_id=1, source_target_pairs={{0,2},{1,3},{2,0},{3,1},{4,6},{5,7},{6,4},{7,5},{8,10},{9,11},{10,... | collective-permute-start | bytes 663560 | tf_op jit(solution)/shard_map/ppermute | solution.py:39
  34.2 7.6 %collective-permute-done.7 = bf16[48,2304]{1,0:T(8,128)(2,1)S(1)} collective-permute-done((bf16[48,2304]{1,0:T(8,128)(2,1)S(1)}, bf16[48,2304]{1,0:T(8,128)(2,1)S(1)}, u32[]{:S(2)}, u32[]{:S(2)}) %collective-permute-start.7) | collective-permute-done | bytes 221216 | tf_op jit(solution)/shard_map/ppermute | solution.py:39
  42.8 7.3 %collective-permute-done.4 = bf16[192,1152]{1,0:T(8,128)(2,1)S(1)} collective-permute-done((bf16[192,1152]{1,0:T(8,128)(2,1)S(1)}, bf16[192,1152]{1,0:T(8,128)(2,1)S(1)}, u32[]{:S(2)}, u32[]{:S(2)}) %collective-permute-start.4) | collective-permute-done | bytes 442400 | tf_op jit(solution)/shard_map/ppermute | solution.py:39
  60.9 5.1 %shard_map.305 = (bf16[64,1536]{1,0:T(8,128)(2,1)}, bf16[64,1536]{1,0:T(8,128)(2,1)}, bf16[768,2304]{1,0:T(8,128)(2,1)}) custom-call(s32[3]{0:T(128)} %pad_add_fusion.place_ref, bf16[128,768]{1,0:T(8,128)(2,1)} %pad_maximum_fusion.9.x_ref, f32[2,768]{1,0:T(2,128)} %reshape.111.gain_ref, f32[128,128]{1,0:T(8,128)} %pad_maximum_fusion.10.cos_ref, ...), custom_call_target="tpu_custom_call" | custom-call | flops 4718592 | bytes 119808 | tf_op jit(solution)/shard_map/pallas_call | solution.py:687
  67.3 4.9 %collective-permute-start.11 = (bf16[64,1536]{1,0:T(8,128)(2,1)}, bf16[64,1536]{1,0:T(8,128)(2,1)S(1)}, u32[]{:S(2)}, u32[]{:S(2)}) collective-permute-start(bf16[64,1536]{1,0:T(8,128)(2,1)} %get-tuple-element.92), channel_id=1, source_target_pairs={{0,1},{1,2},{2,3},{3,4},{4,5},{5,6},{6,7},{7,8},{8,9},{9,10},{10,1... | collective-permute-start | bytes 589832 | tf_op jit(solution)/shard_map/ppermute | solution.py:164
  73.5 10.1 %shard_map.306 = (bf16[1280,768]{1,0:T(8,128)(2,1)}, bf16[1280,768]{1,0:T(8,128)(2,1)}, bf16[1280,768]{1,0:T(8,128)(2,1)}, bf16[1280,768]{1,0:T(8,128)(2,1)}) custom-call(bf16[1280,768]{1,0:T(8,128)(2,1)} %x_ref.4, f32[2,768]{1,0:T(2,128)} %reshape.111.gain_ref, bf16[768,2304]{1,0:T(8,128)(2,1)} %get-tuple-element.87.w_ref, f32[1280,128]{1,0:T(8,128)} %copy-done.3, ...), custom_call_target="tpu_custom_call" | custom-call | flops 70778880 | bytes 208896 | tf_op jit(solution)/shard_map/pallas_call | solution.py:673
  84.3 17.0 %shard_map.307 = (bf16[768,1280]{1,0:T(8,128)(2,1)}, f32[6,20,128]{2,1,0:T(8,128)}) custom-call(s32[3]{0:T(128)} %pad_add_fusion.1.meta_ref, bf16[1280,768]{1,0:T(8,128)(2,1)} %get-tuple-element.99.q_ref, bf16[1280,768]{1,0:T(8,128)(2,1)} %get-tuple-element.90.k_ref, bf16[1280,768]{1,0:T(8,128)(2,1)} %get-tuple-element.91.v_ref, bf16[64,1536]{1,0:T(8,128)(2,1)} %copy-done.1, ...), custom_call_target="tpu_custom_call" | custom-call | flops 31457280 | bytes 122880 | tf_op jit(solution)/shard_map/pallas_call | solution.py:719
  106.7 16.9 %shard_map.308 = (bf16[768,1280]{1,0:T(8,128)(2,1)}, f32[6,20,128]{2,1,0:T(8,128)}) custom-call(s32[3]{0:T(128)} %pad_add_fusion.1.meta_ref, bf16[1280,768]{1,0:T(8,128)(2,1)} %get-tuple-element.99.q_ref, bf16[1280,768]{1,0:T(8,128)(2,1)} %get-tuple-element.90.k_ref, ...), custom_call_target="tpu_custom_call", output_to_operand_aliasing={{0}: (8, {}), {1}: (9, {})} | custom-call | flops 31457280 | bytes 122880 | tf_op jit(solution)/shard_map/pallas_call | solution.py:719
  123.7 59.5 %shard_map.309 = (bf16[1280,768]{1,0:T(8,128)(2,1)}, bf16[1280,768]{1,0:T(8,128)(2,1)}, bf16[1280,768]{1,0:T(8,128)(2,1)}, bf16[768,2304]{1,0:T(8,128)(2,1)}, bf16[768,2304]{1,0:T(8,128)(2,1)}) custom-call(s32[3]{0:T(128)} %pad_add_fusion.place_ref, bf16[1280,768]{1,0:T(8,128)(2,1)} %x_ref.4, bf16[768,1280]{1,0:T(8,128)(2,1)} %get-tuple-element.101.o_ref, ...), custom_call_target="tpu_custom_call" | custom-call | flops 353894400 | bytes 399360 | tf_op jit(solution)/shard_map/pallas_call | solution.py:798
  184.2 11.3 %shard_map.310 = (bf16[256,768]{1,0:T(8,128)(2,1)}, f32[512,768]{1,0:T(8,128)}, f32[512,768]{1,0:T(8,128)}, bf16[2,64,768]{2,1,0:T(8,128)(2,1)}, bf16[2,64,768]{...) custom-call(s32[3]{0:T(128)} %pad_add_fusion.1.meta_ref, bf16[1280,768]{1,0:T(8,128)(2,1)} %get-tuple-element.99.q_ref, ...), custom_call_target="tpu_custom_call" | custom-call | flops 15728640 | bytes 153600 | tf_op jit(solution)/shard_map/pallas_call | solution.py:756
  197.3 3.9 %add_convert_fusion = bf16[768,2304]{1,0:T(8,128)(2,1)S(1)} fusion(bf16[768,2304]{1,0:T(8,128)(2,1)} %copy-done.9, bf16[768,2304]{1,0:T(8,128)(2,1)} %get-tuple-element.105), kind=kLoop, calls=%fused_computation | loop fusion | flops 7077888 | bytes 10616832 | tf_op jit(solution)/shard_map/convert_element_type | solution.py:118
  207.5 5.2 %collective-permute-start.17 = (bf16[2,64,768]{2,1,0:T(8,128)(2,1)}, bf16[2,64,768]{2,1,0:T(8,128)(2,1)}, u32[]{:S(2)}, u32[]{:S(2)}) collective-permute-start(bf16[2,64,768]{2,1,0:T(8,128)(2,1)} %get-tuple-element.120), channel_id=1, source_target_pairs={{0,1},{1,2},{2,3},{3,4},{4,5},{5,6},{6,7},{7,8},{8,9},{9,10},{10,1... | collective-permute-start | bytes 589832 | tf_op jit(solution)/shard_map/ppermute | solution.py:164
  212.8 28.2 %shard_map.311 = (bf16[1280,768]{1,0:T(8,128)(2,1)}, bf16[1280,768]{1,0:T(8,128)(2,1)}, bf16[1280,768]{1,0:T(8,128)(2,1)}) custom-call(s32[3]{0:T(128)} %pad_add_fusion.1.meta_ref, bf16[1280,768]{1,0:T(8,128)(2,1)} %get-tuple-element.99.q_ref, bf16[1280,768]{1,0:T(8,128)(2,1)} %get-tuple-element.90.k_ref, bf16[1280,768]{1,0:T(8,128)(2,1)} %get-tuple-element.91.v_ref, ...), custom_call_target="tpu_custom_call" | custom-call | flops 78643200 | bytes 215040 | tf_op jit(solution)/shard_map/pallas_call | solution.py:778
  241.0 11.7 %shard_map.312 = (bf16[128,768]{1,0:T(8,128)(2,1)}, bf16[128,768]{1,0:T(8,128)(2,1)}, bf16[768,1152]{1,0:T(8,128)(2,1)}, bf16[768,1152]{1,0:T(8,128)(2,1)}) custom-call(s32[3]{0:T(128)} %pad_add_fusion.place_ref, bf16[1280,768]{1,0:T(8,128)(2,1)} %get-tuple-element.115.h_ref, bf16[1280,768]{1,0:T(8,128)(2,1)} %get-tuple-element.129.dq_ref, ...), custom_call_target="tpu_custom_call" | custom-call | flops 70778880 | bytes 178176 | tf_op jit(solution)/shard_map/pallas_call | solution.py:822
  252.8 3.2 fusion.8
  257.4 3.3 %collective-permute-done.22 = bf16[768,1152]{1,0:T(8,128)(2,1)S(1)} collective-permute-done((bf16[768,1152]{1,0:T(8,128)(2,1)S(1)}, bf16[768,1152]{1,0:T(8,128)(2,1)S(1)}, u32[]{:S(2)}, u32[]{:S(2)}) %collective-permute-start.22) | collective-permute-done | bytes 1769504 | tf_op jit(solution)/shard_map/ppermute | solution.py:39
  262.2 2.0 collective-permute-start.23
  266.6 4.9 %collective-permute-start.28 = (bf16[48,2304]{1,0:T(8,128)(2,1)}, bf16[48,2304]{1,0:T(8,128)(2,1)S(1)}, u32[]{:S(2)}, u32[]{:S(2)}) collective-permute-start(bf16[48,2304]{1,0:T(8,128)(2,1)} %get-tuple-element.186), channel_id=1, source_target_pairs={{0,2},{1,3},{2,0},{3,1},{4,6},{5,7},{6,4},{7,5},{8,10},{9,11},{10,... | collective-permute-start | bytes 663560 | tf_op jit(solution)/shard_map/ppermute | solution.py:39
  271.5 11.3 %shard_map.313 = bf16[1280,768]{1,0:T(8,128)(2,1)} custom-call(bf16[1280,768]{1,0:T(8,128)(2,1)} %x_ref.4, f32[2,768]{1,0:T(2,128)} %reshape.111.gain_ref, bf16[768,2304]{1,0:T(8,128)(2,1)} %get-tuple-element.87.w_ref, bf16[1280,768]{1,0:T(8,128)(2,1)} %get-tuple-element.103.dmid_ref, bf16[1280,768]{1,0:T(8,128)(2,1)} %get-tuple-element.129.dq_ref, ...), custom_call_target="tpu_custom_call" | custom-call | flops 70778880 | bytes 270336 | tf_op jit(solution)/shard_map/pallas_call | solution.py:841
  282.9 3.2 collective-permute-done.24
  287.4 4.2 %collective-permute-done.29 = bf16[48,2304]{1,0:T(8,128)(2,1)S(1)} collective-permute-done((bf16[48,2304]{1,0:T(8,128)(2,1)}, bf16[48,2304]{1,0:T(8,128)(2,1)S(1)}, u32[]{:S(2)}, u32[]{:S(2)}) %collective-permute-start.29) | collective-permute-done | bytes 221216 | tf_op jit(solution)/shard_map/ppermute | solution.py:39
  291.6 3.1 collective-permute-start.26
  294.7 2.4 collective-permute-start.31
  300.8 4.0 %collective-permute-done.30 = bf16[48,1152]{1,0:T(8,128)(2,1)S(1)} collective-permute-done((bf16[48,1152]{1,0:T(8,128)(2,1)S(1)}, bf16[48,1152]{1,0:T(8,128)(2,1)S(1)}, u32[]{:S(2)}, u32[]{:S(2)}) %collective-permute-start.30) | collective-permute-done | bytes 110624 | tf_op jit(solution)/shard_map/ppermute | solution.py:39
  308.5 2.0 collective-permute-done.34
  315.9 3.4 %multiply_subtract_fusion = (f32[192,2304]{1,0:T(8,128)}, f32[192,2304]{1,0:T(8,128)}, f32[192,2304]{1,0:T(8,128)}, f32[192]{0:T(256)S(1)}) fusion(f32[192,2304]{1,0:T(8,128)S(1)} %copy-done.5, bf16[192,1152]{1,0:T(8,128)(2,1)S(1)} %slice.122, bf16[192,1152]{1,0:T(8,128)(2,1)S(1)} %slice.121, f32[192,2304]{1,0:T(8,128)S(1)} %copy-done.12, ...), kind=kLoop, calls=%fused_computation.20 | loop fusion | flops 10174272 | bytes 11502336 | tf_op jit(solution)/shard_map/sub | solution.py:871
  321.7 2.0 multiply_subtract_fusion.2
  325.3 3.4 %multiply_subtract_fusion.1 = (f32[192,2304]{1,0:T(8,128)}, f32[192,2304]{1,0:T(8,128)}, f32[192,2304]{1,0:T(8,128)}, f32[192]{0:T(256)S(1)}) fusion(f32[192,2304]{1,0:T(8,128)S(1)} %copy-done.6, bf16[192,1152]{1,0:T(8,128)(2,1)S(1)} %get-tuple-element.183, bf16[192,1152]{1,0:T(8,128)(2,1)S(1)} %get-tuple-element.182, f32[192,2304]{1,0:T(8,128)S(1)} %copy-done.14, ...), kind=kLoop, calls=%fused_computation.21 | loop fusion | flops 10174272 | bytes 11502336 | tf_op jit(solution)/shard_map/sub | solution.py:871
  (207 shorter events, 72.0 us)
Async XLA Ops:
  5.7 15.9 %collective-permute-start = (bf16[56,1152]{1,0:T(8,128)(2,1)}, bf16[56,1152]{1,0:T(8,128)(2,1)}, u32[]{:S(2)}, u32[]{:S(2)}) collective-permute-start(bf16[56,1152]{1,0:T(8,128)(2,1)} %fusion.24), channel_id=1, source_target_pairs={{0,1},{1,0},{2,3},{3,2},{4,5},{5,4},{6,7},{7,6},{8,9},{9,8},{10,11... | collective-permute-start | bytes 387080 | tf_op jit(solution)/shard_map/ppermute | solution.py:39
  8.7 18.3 %collective-permute-start.1 = (bf16[56,1152]{1,0:T(8,128)(2,1)}, bf16[56,1152]{1,0:T(8,128)(2,1)}, u32[]{:S(2)}, u32[]{:S(2)}) collective-permute-start(bf16[56,1152]{1,0:T(8,128)(2,1)} %fusion.24), channel_id=1, source_target_pairs={{0,2},{1,3},{2,0},{3,1},{4,6},{5,7},{6,4},{7,5},{8,10},{9,11},{10,... | collective-permute-start | bytes 387080 | tf_op jit(solution)/shard_map/ppermute | solution.py:39
  11.3 16.6 %collective-permute-start.2 = (bf16[56,1152]{1,0:T(8,128)(2,1)}, bf16[56,1152]{1,0:T(8,128)(2,1)}, u32[]{:S(2)}, u32[]{:S(2)}) collective-permute-start(bf16[56,1152]{1,0:T(8,128)(2,1)} %fusion.24), channel_id=1, source_target_pairs={{0,3},{1,2},{2,1},{3,0},{4,7},{5,6},{6,5},{7,4},{8,11},{9,10},{10,... | collective-permute-start | bytes 387080 | tf_op jit(solution)/shard_map/ppermute | solution.py:39
  21.6 11.2 %collective-permute-start.6 = (bf16[48,2304]{1,0:T(8,128)(2,1)S(1)}, bf16[48,2304]{1,0:T(8,128)(2,1)S(1)}, u32[]{:S(2)}, u32[]{:S(2)}) collective-permute-start(bf16[48,2304]{1,0:T(8,128)(2,1)S(1)} %pad_maximum_fusion.6), channel_id=1, source_target_pairs={{0,1},{1,0},{2,3},{3,2},{4,5},{5,4},{6,7},{7,6},{8,9},{9,8},{10,11... | collective-permute-start | bytes 663560 | tf_op jit(solution)/shard_map/ppermute | solution.py:39
  22.5 19.3 %collective-permute-start.7 = (bf16[48,2304]{1,0:T(8,128)(2,1)S(1)}, bf16[48,2304]{1,0:T(8,128)(2,1)S(1)}, u32[]{:S(2)}, u32[]{:S(2)}) collective-permute-start(bf16[48,2304]{1,0:T(8,128)(2,1)S(1)} %pad_maximum_fusion.6), channel_id=1, source_target_pairs={{0,2},{1,3},{2,0},{3,1},{4,6},{5,7},{6,4},{7,5},{8,10},{9,11},{10,... | collective-permute-start | bytes 663560 | tf_op jit(solution)/shard_map/ppermute | solution.py:39
  26.0 15.8 %collective-permute-start.8 = (bf16[48,2304]{1,0:T(8,128)(2,1)S(1)}, bf16[48,2304]{1,0:T(8,128)(2,1)S(1)}, u32[]{:S(2)}, u32[]{:S(2)}) collective-permute-start(bf16[48,2304]{1,0:T(8,128)(2,1)S(1)} %pad_maximum_fusion.6), channel_id=1, source_target_pairs={{0,3},{1,2},{2,1},{3,0},{4,7},{5,6},{6,5},{7,4},{8,11},{9,10},{10,... | collective-permute-start | bytes 663560 | tf_op jit(solution)/shard_map/ppermute | solution.py:39
  28.9 14.0 %collective-permute-start.3 = (bf16[192,1152]{1,0:T(8,128)(2,1)S(1)}, bf16[192,1152]{1,0:T(8,128)(2,1)S(1)}, u32[]{:S(2)}, u32[]{:S(2)}) collective-permute-start(bf16[192,1152]{1,0:T(8,128)(2,1)S(1)} %pad_maximum_fusion.3), channel_id=1, source_target_pairs={{0,8},{4,12},{8,0},{12,4},{16,24},{20,28},{24,16},{28,20},{1,9},{5... | collective-permute-start | bytes 1327112 | tf_op jit(solution)/shard_map/ppermute | solution.py:39
  30.6 19.5 %collective-permute-start.4 = (bf16[192,1152]{1,0:T(8,128)(2,1)S(1)}, bf16[192,1152]{1,0:T(8,128)(2,1)S(1)}, u32[]{:S(2)}, u32[]{:S(2)}) collective-permute-start(bf16[192,1152]{1,0:T(8,128)(2,1)S(1)} %pad_maximum_fusion.3), channel_id=1, source_target_pairs={{0,16},{4,20},{8,24},{12,28},{16,0},{20,4},{24,8},{28,12},{1,17},{... | collective-permute-start | bytes 1327112 | tf_op jit(solution)/shard_map/ppermute | solution.py:39
  32.7 17.5 %collective-permute-start.5 = (bf16[192,1152]{1,0:T(8,128)(2,1)S(1)}, bf16[192,1152]{1,0:T(8,128)(2,1)S(1)}, u32[]{:S(2)}, u32[]{:S(2)}) collective-permute-start(bf16[192,1152]{1,0:T(8,128)(2,1)S(1)} %pad_maximum_fusion.3), channel_id=1, source_target_pairs={{0,24},{4,28},{8,16},{12,20},{16,8},{20,12},{24,0},{28,4},{1,25},{... | collective-permute-start | bytes 1327112 | tf_op jit(solution)/shard_map/ppermute | solution.py:39
  50.3 10.6 %collective-permute-start.9 = (bf16[768,1152]{1,0:T(8,128)(2,1)S(1)}, bf16[768,1152]{1,0:T(8,128)(2,1)}, u32[]{:S(2)}, u32[]{:S(2)}) collective-permute-start(bf16[768,1152]{1,0:T(8,128)(2,1)S(1)} %constant_dynamic-update-slice_fusion.refs_0_), channel_id=1, source_target_pairs={{0,4},{4,0},{8,12},{12,8},{16,20},{20,16},{24,28},{28,24},{1,5},{5... | collective-permute-start | bytes 5308424 | tf_op jit(solution)/shard_map/ppermute | solution.py:39
  55.2 46.1 %collective-permute-start.14 = (bf16[192,2304]{1,0:T(8,128)(2,1)}, bf16[192,2304]{1,0:T(8,128)(2,1)}, u32[]{:S(2)}, u32[]{:S(2)}) collective-permute-start(bf16[192,2304]{1,0:T(8,128)(2,1)} %pad_maximum_fusion), channel_id=1, source_target_pairs={{0,24},{4,28},{8,16},{12,20},{16,8},{20,12},{24,0},{28,4},{1,25},{... | collective-permute-start | bytes 2654216 | tf_op jit(solution)/shard_map/ppermute | solution.py:39
  56.7 44.6 %collective-permute-start.13 = (bf16[192,2304]{1,0:T(8,128)(2,1)}, bf16[192,2304]{1,0:T(8,128)(2,1)}, u32[]{:S(2)}, u32[]{:S(2)}) collective-permute-start(bf16[192,2304]{1,0:T(8,128)(2,1)} %pad_maximum_fusion), channel_id=1, source_target_pairs={{0,16},{4,20},{8,24},{12,28},{16,0},{20,4},{24,8},{28,12},{1,17},{... | collective-permute-start | bytes 2654216 | tf_op jit(solution)/shard_map/ppermute | solution.py:39
  57.8 43.5 %collective-permute-start.10 = (bf16[192,2304]{1,0:T(8,128)(2,1)}, bf16[192,2304]{1,0:T(8,128)(2,1)}, u32[]{:S(2)}, u32[]{:S(2)}) collective-permute-start(bf16[192,2304]{1,0:T(8,128)(2,1)} %pad_maximum_fusion), channel_id=1, source_target_pairs={{0,8},{4,12},{8,0},{12,4},{16,24},{20,28},{24,16},{28,20},{1,9},{5... | collective-permute-start | bytes 2654216 | tf_op jit(solution)/shard_map/ppermute | solution.py:39
  66.0 17.6 %collective-permute-start.12 = (bf16[64,1536]{1,0:T(8,128)(2,1)}, bf16[64,1536]{1,0:T(8,128)(2,1)S(1)}, u32[]{:S(2)}, u32[]{:S(2)}) collective-permute-start(bf16[64,1536]{1,0:T(8,128)(2,1)} %get-tuple-element.85), channel_id=1, source_target_pairs={{1,0},{2,1},{3,2},{4,3},{5,4},{6,5},{7,6},{8,7},{9,8},{10,9},{11,1... | collective-permute-start | bytes 589832 | tf_op jit(solution)/shard_map/ppermute | solution.py:170
  67.3 16.3 %collective-permute-start.11 = (bf16[64,1536]{1,0:T(8,128)(2,1)}, bf16[64,1536]{1,0:T(8,128)(2,1)S(1)}, u32[]{:S(2)}, u32[]{:S(2)}) collective-permute-start(bf16[64,1536]{1,0:T(8,128)(2,1)} %get-tuple-element.92), channel_id=1, source_target_pairs={{0,1},{1,2},{2,3},{3,4},{4,5},{5,6},{6,7},{7,8},{8,9},{9,10},{10,1... | collective-permute-start | bytes 589832 | tf_op jit(solution)/shard_map/ppermute | solution.py:164
  105.0 18.6 %collective-permute-start.15 = (bf16[768,2304]{1,0:T(8,128)(2,1)S(1)}, bf16[768,2304]{1,0:T(8,128)(2,1)}, u32[]{:S(2)}, u32[]{:S(2)}) collective-permute-start(bf16[768,2304]{1,0:T(8,128)(2,1)S(1)} %constant_dynamic-update-slice_fusion.7.refs_0_), channel_id=1, source_target_pairs={{0,4},{4,0},{8,12},{12,8},{16,20},{20,16},{24,28},{28,24},{1,5},{5... | collective-permute-start | bytes 10616840 | tf_op jit(solution)/shard_map/ppermute | solution.py:39
  183.2 12.3 %collective-permute-start.16 = (bf16[768,2304]{1,0:T(8,128)(2,1)}, bf16[768,2304]{1,0:T(8,128)(2,1)S(1)}, u32[]{:S(2)}, u32[]{:S(2)}) collective-permute-start(bf16[768,2304]{1,0:T(8,128)(2,1)} %get-tuple-element.106), channel_id=1, source_target_pairs={{0,4},{4,0},{8,12},{12,8},{16,20},{20,16},{24,28},{28,24},{1,5},{5... | collective-permute-start | bytes 10616840 | tf_op jit(solution)/shard_map/ppermute | solution.py:39
  202.7 50.0 %collective-permute-start.19 = (bf16[4,48,2304]{2,1,0:T(8,128)(2,1)}, bf16[4,48,2304]{2,1,0:T(8,128)(2,1)}, u32[]{:S(2)}, u32[]{:S(2)}) collective-permute-start(bf16[4,48,2304]{2,1,0:T(8,128)(2,1)} %get-tuple-element.170), channel_id=1, source_target_pairs={{0,8},{4,12},{8,0},{12,4},{16,24},{20,28},{24,16},{28,20},{1,9},{5... | collective-permute-start | bytes 2654216 | tf_op jit(solution)/shard_map/ppermute | solution.py:39
  203.8 48.9 %collective-permute-start.20 = (bf16[4,48,2304]{2,1,0:T(8,128)(2,1)}, bf16[4,48,2304]{2,1,0:T(8,128)(2,1)}, u32[]{:S(2)}, u32[]{:S(2)}) collective-permute-start(bf16[4,48,2304]{2,1,0:T(8,128)(2,1)} %get-tuple-element.172), channel_id=1, source_target_pairs={{0,16},{4,20},{8,24},{12,28},{16,0},{20,4},{24,8},{28,12},{1,17},{... | collective-permute-start | bytes 2654216 | tf_op jit(solution)/shard_map/ppermute | solution.py:39
  205.0 47.7 %collective-permute-start.21 = (bf16[4,48,2304]{2,1,0:T(8,128)(2,1)}, bf16[4,48,2304]{2,1,0:T(8,128)(2,1)}, u32[]{:S(2)}, u32[]{:S(2)}) collective-permute-start(bf16[4,48,2304]{2,1,0:T(8,128)(2,1)} %get-tuple-element.171), channel_id=1, source_target_pairs={{0,24},{4,28},{8,16},{12,20},{16,8},{20,12},{24,0},{28,4},{1,25},{... | collective-permute-start | bytes 2654216 | tf_op jit(solution)/shard_map/ppermute | solution.py:39
  206.2 34.7 %collective-permute-start.18 = (bf16[2,64,768]{2,1,0:T(8,128)(2,1)}, bf16[2,64,768]{2,1,0:T(8,128)(2,1)}, u32[]{:S(2)}, u32[]{:S(2)}) collective-permute-start(bf16[2,64,768]{2,1,0:T(8,128)(2,1)} %get-tuple-element.108), channel_id=1, source_target_pairs={{1,0},{2,1},{3,2},{4,3},{5,4},{6,5},{7,6},{8,7},{9,8},{10,9},{11,1... | collective-permute-start | bytes 589832 | tf_op jit(solution)/shard_map/ppermute | solution.py:170
  207.5 33.4 %collective-permute-start.17 = (bf16[2,64,768]{2,1,0:T(8,128)(2,1)}, bf16[2,64,768]{2,1,0:T(8,128)(2,1)}, u32[]{:S(2)}, u32[]{:S(2)}) collective-permute-start(bf16[2,64,768]{2,1,0:T(8,128)(2,1)} %get-tuple-element.120), channel_id=1, source_target_pairs={{0,1},{1,2},{2,3},{3,4},{4,5},{5,6},{6,7},{7,8},{8,9},{9,10},{10,1... | collective-permute-start | bytes 589832 | tf_op jit(solution)/shard_map/ppermute | solution.py:164
  262.2 20.6 %collective-permute-start.23 = (bf16[4,48,1152]{2,1,0:T(8,128)(2,1)}, bf16[4,48,1152]{2,1,0:T(8,128)(2,1)S(1)}, u32[]{:S(2)}, u32[]{:S(2)}) collective-permute-start(bf16[4,48,1152]{2,1,0:T(8,128)(2,1)} %get-tuple-element.177), channel_id=1, source_target_pairs={{0,8},{4,12},{8,0},{12,4},{16,24},{20,28},{24,16},{28,20},{1,9},{5... | collective-permute-start | bytes 1327112 | tf_op jit(solution)/shard_map/ppermute | solution.py:39
  264.2 21.8 %collective-permute-start.24 = (bf16[4,48,1152]{2,1,0:T(8,128)(2,1)}, bf16[4,48,1152]{2,1,0:T(8,128)(2,1)S(1)}, u32[]{:S(2)}, u32[]{:S(2)}) collective-permute-start(bf16[4,48,1152]{2,1,0:T(8,128)(2,1)} %get-tuple-element.179), channel_id=1, source_target_pairs={{0,16},{4,20},{8,24},{12,28},{16,0},{20,4},{24,8},{28,12},{1,17},{... | collective-permute-start | bytes 1327112 | tf_op jit(solution)/shard_map/ppermute | solution.py:39
  264.4 21.7 %collective-permute-start.25 = (bf16[4,48,1152]{2,1,0:T(8,128)(2,1)}, bf16[4,48,1152]{2,1,0:T(8,128)(2,1)}, u32[]{:S(2)}, u32[]{:S(2)}) collective-permute-start(bf16[4,48,1152]{2,1,0:T(8,128)(2,1)} %get-tuple-element.178), channel_id=1, source_target_pairs={{0,24},{4,28},{8,16},{12,20},{16,8},{20,12},{24,0},{28,4},{1,25},{... | collective-permute-start | bytes 1327112 | tf_op jit(solution)/shard_map/ppermute | solution.py:39
  266.6 20.7 %collective-permute-start.27 = (bf16[48,2304]{1,0:T(8,128)(2,1)}, bf16[48,2304]{1,0:T(8,128)(2,1)S(1)}, u32[]{:S(2)}, u32[]{:S(2)}) collective-permute-start(bf16[48,2304]{1,0:T(8,128)(2,1)} %get-tuple-element.184), channel_id=1, source_target_pairs={{0,1},{1,0},{2,3},{3,2},{4,5},{5,4},{6,7},{7,6},{8,9},{9,8},{10,11... | collective-permute-start | bytes 663560 | tf_op jit(solution)/shard_map/ppermute | solution.py:39
  266.6 20.7 %collective-permute-start.28 = (bf16[48,2304]{1,0:T(8,128)(2,1)}, bf16[48,2304]{1,0:T(8,128)(2,1)S(1)}, u32[]{:S(2)}, u32[]{:S(2)}) collective-permute-start(bf16[48,2304]{1,0:T(8,128)(2,1)} %get-tuple-element.186), channel_id=1, source_target_pairs={{0,2},{1,3},{2,0},{3,1},{4,6},{5,7},{6,4},{7,5},{8,10},{9,11},{10,... | collective-permute-start | bytes 663560 | tf_op jit(solution)/shard_map/ppermute | solution.py:39
  294.7 10.1 %collective-permute-start.30 = (bf16[48,1152]{1,0:T(8,128)(2,1)S(1)}, bf16[48,1152]{1,0:T(8,128)(2,1)S(1)}, u32[]{:S(2)}, u32[]{:S(2)}) collective-permute-start(bf16[48,1152]{1,0:T(8,128)(2,1)S(1)} %get-tuple-element.193), channel_id=1, source_target_pairs={{0,2},{1,3},{2,0},{3,1},{4,6},{5,7},{6,4},{7,5},{8,10},{9,11},{10,... | collective-permute-start | bytes 331784 | tf_op jit(solution)/shard_map/ppermute | solution.py:39
  294.7 10.1 %collective-permute-start.31 = (bf16[48,1152]{1,0:T(8,128)(2,1)S(1)}, bf16[48,1152]{1,0:T(8,128)(2,1)S(1)}, u32[]{:S(2)}, u32[]{:S(2)}) collective-permute-start(bf16[48,1152]{1,0:T(8,128)(2,1)S(1)} %get-tuple-element.192), channel_id=1, source_target_pairs={{0,3},{1,2},{2,1},{3,0},{4,7},{5,6},{6,5},{7,4},{8,11},{9,10},{10,... | collective-permute-start | bytes 331784 | tf_op jit(solution)/shard_map/ppermute | solution.py:39
  297.2 10.7 %collective-permute-start.35 = (bf16[48,2304]{1,0:T(8,128)(2,1)S(1)}, bf16[48,2304]{1,0:T(8,128)(2,1)S(1)}, u32[]{:S(2)}, u32[]{:S(2)}) collective-permute-start(bf16[48,2304]{1,0:T(8,128)(2,1)S(1)} %get-tuple-element.165), channel_id=1, source_target_pairs={{0,24},{4,28},{8,16},{12,20},{16,8},{20,12},{24,0},{28,4},{1,25},{... | collective-permute-start | bytes 663560 | tf_op jit(solution)/shard_map/ppermute | solution.py:39
  298.8 11.7 %collective-permute-start.34 = (bf16[48,2304]{1,0:T(8,128)(2,1)S(1)}, bf16[48,2304]{1,0:T(8,128)(2,1)S(1)}, u32[]{:S(2)}, u32[]{:S(2)}) collective-permute-start(bf16[48,2304]{1,0:T(8,128)(2,1)S(1)} %get-tuple-element.165), channel_id=1, source_target_pairs={{0,16},{4,20},{8,24},{12,28},{16,0},{20,4},{24,8},{28,12},{1,17},{... | collective-permute-start | bytes 663560 | tf_op jit(solution)/shard_map/ppermute | solution.py:39
  313.1 10.5 %collective-permute-start.38 = (bf16[192,1152]{1,0:T(8,128)(2,1)S(1)}, bf16[192,1152]{1,0:T(8,128)(2,1)S(1)}, u32[]{:S(2)}, u32[]{:S(2)}) collective-permute-start(bf16[192,1152]{1,0:T(8,128)(2,1)S(1)} %bitcast.97), channel_id=1, source_target_pairs={{0,4},{4,0},{8,12},{12,8},{16,20},{20,16},{24,28},{28,24},{1,5},{5... | collective-permute-start | bytes 1327112 | tf_op jit(solution)/shard_map/ppermute | solution.py:39
  (38 other events, 235.4 us)
where the time goes:
time: 329 us; the launch traced here: 330 us
  Pallas kernels  171 us (52%)
  starting transfers between devices  59.9 us (18%)
  other arithmetic  34.1 us (10%)
  waiting for transfers between devices  34.1 us (10%)
  local copies, waits for them, and re-layouts  28.7 us (9%)
    pallas_call x1, Pallas kernels, middle(): call(functools.partial(middle_kernel, split), rows // tile, [pl.BlockSpec...  59.5 us
    ppermute x36, starting transfers between devices, swap(): return lax.ppermute(value, axis, [(i, i ^ flip) for i in range(count)])  47.2 us
    ppermute x36, waiting for transfers between devices, swap(): return lax.ppermute(value, axis, [(i, i ^ flip) for i in range(count)])  34.1 us
    pallas_call x2, Pallas kernels, attend(): call(attend_kernel, count, [pl.BlockSpec(memory_space=pltpu.SMEM)] + [col...  33.9 us
    pallas_call x1, Pallas kernels, attend_back(): call(attend_back_kernel, steps, back_specs(rows, steps) + [pairs(2 * PAIR...  28.2 us
    unnamed x66, local copies, waits for them, and re-layouts  12.4 us
    pallas_call x1, Pallas kernels, qkv_gradient(): call(functools.partial(qkv_grad_kernel, split), rows // tile, [pl.BlockSp...  11.7 us
    pallas_call x1, Pallas kernels, attend_back_edges(): call(attend_back_edges_kernel, steps, back_specs(rows, steps), [pairs(2 *...  11.3 us
  transfers between devices with their start and end apart: 40, of which 9 were waited for; matrix products, arithmetic and copies ran while one was open for 10% of the time, Pallas kernels for 34%

commit v1 on v0

--- a/solution.py
+++ b/solution.py
@@ -12,11 +12,11 @@
 HALF = 64
 ADAM_STEP = 5
 LANES = 128
-ROWS = 64
+ROWS = 128
 SPAN = ROWS + 2 * HALF
-PAIR = 2 * ROWS
 TILE = 256
 WIDE_TILE = 640
+GROUP = 2
 
 
 norm_epsilon = 1e-05
@@ -212,9 +212,9 @@
 
 def mask_bias(meta_ref, block):
     first = block * ROWS
-    shape = (SPAN, LANES)
+    shape = (SPAN, ROWS)
     key = lax.broadcasted_iota(jnp.int32, shape, 0) + (first - HALF)
-    query = lax.broadcasted_iota(jnp.int32, shape, 1) % ROWS + first
+    query = lax.broadcasted_iota(jnp.int32, shape, 1) + first
     start, low, high = meta_ref[0], meta_ref[1], meta_ref[2]
     apart = jnp.abs(query - key) > HALF
     other = (query >= start) != (key >= start)
@@ -230,20 +230,13 @@
     )
 
 
-def unstacked(even, odd):
-    lane = lax.broadcasted_iota(jnp.int32, (64, LANES), 1)
-    top = jnp.where(lane < ROWS, even[:64], pltpu.roll(odd[:64], ROWS, 1))
-    bottom = jnp.where(lane < ROWS, pltpu.roll(even[64:], ROWS, 1), odd[64:])
-    return jnp.concatenate([top, bottom], axis=0)
+def unstacked(values):
+    depth = lax.broadcasted_iota(jnp.int32, (LANES, ROWS), 0)
+    return jnp.where(depth < 64, values[:, :ROWS], values[:, ROWS:])
 
 
 def window(block):
     return slice(block * ROWS, block * ROWS + SPAN)
-
-
-def turned_window(kt, kt_odd, block):
-    at = (block // 2) * PAIR
-    return (kt_odd if block % 2 else kt)[:, at : at + SPAN]
 
 
 def assemble(place_ref, shards, quarters, copy):
@@ -318,16 +311,15 @@
     dst[HALF + rows :, :] = right[...]
 
 
-def flip(dst, src, start, stop, shift):
+def flip(dst, src, start, stop):
     for at in range(start, stop, LANES):
-        end = min(at + LANES, stop)
-        dst[:, at - shift : end - shift] = src[at:end, :].T
+        dst[:, at : at + LANES] = src[at : at + LANES, :].T
 
 
 def attend_kernel(
     meta_ref, q_ref, k_ref, v_ref, kl_ref, vl_ref, kr_ref, vr_ref, *refs
 ):
-    o_ref, lse_ref, kx, vx, bias, vt, vt_odd = refs[-7:]
+    o_ref, lse_ref, kx, vx, bias, vt = refs[-6:]
     blocks = q_ref.shape[0] // ROWS
 
     @pl.when(pl.program_id(0) == 0)
@@ -337,73 +329,85 @@
 
     fill(kx, kl_ref, k_ref, kr_ref)
     fill(vx, vl_ref, v_ref, vr_ref)
-    flip(vt, vx, 0, vx.shape[0], 0)
-    flip(vt_odd, vx, ROWS, vx.shape[0], ROWS)
-    outs = []
-    for n in range(blocks):
-        queries = stacked(q_ref[n * ROWS : (n + 1) * ROWS, :])
-        scores = dot_rows(kx[window(n), :], queries) + bias[n]
-        top = jnp.max(scores, axis=0, keepdims=True)
-        weights = jnp.exp(scores - top)
-        total = jnp.sum(weights, axis=0, keepdims=True)
-        out = dot(turned_window(vt, vt_odd, n), weights.astype(bf16))
-        outs.append(out * (1.0 / total))
-        lse_ref[0, n : n + 1, :] = top + jnp.log(total)
-        if n % 2:
-            at = (n // 2) * PAIR
-            o_ref[:, at : at + PAIR] = unstacked(*outs[-2:]).astype(bf16)
+    flip(vt, vx, 0, vx.shape[0])
+    for first in range(0, blocks, GROUP):
+        group = range(first, min(first + GROUP, blocks))
+        scores = []
+        for n in group:
+            queries = stacked(q_ref[n * ROWS : (n + 1) * ROWS, :])
+            mask = bias[n]
+            score = dot_rows(kx[window(n), :], queries)
+            scores.append(score + jnp.concatenate([mask, mask], axis=1))
+        tops = [jnp.max(score, axis=0, keepdims=True) for score in scores]
+        weights = [jnp.exp(score - top) for score, top in zip(scores, tops)]
+        totals = [jnp.sum(weight, axis=0, keepdims=True) for weight in weights]
+        outs = [dot(vt[:, window(n)], weight.astype(bf16)) for n, weight in zip(group, weights)]
+        for n, out, top, total in zip(group, outs, tops, totals):
+            own = slice(n * ROWS, (n + 1) * ROWS)
+            o_ref[:, own] = unstacked(out * (1.0 / total)).astype(bf16)
+            lse_ref[0, n : n + 1, :] = top + jnp.log(total)
 
 
 def back_blocks(
-    halves, dq_at, q_ref, do_ref, kx, vx, bias, kt, kt_odd, lse_ref, cos_ref, sin_ref, dq_ref, dkx, dvx
+    blocks, dq_at, q_ref, do_ref, kx, vx, bias, kt, lse_ref, cos_ref, sin_ref, dq_ref, dkx, dvx
 ):
-    for m in halves:
-        outs = []
-        for n in (2 * m, 2 * m + 1):
-            own = slice(n * ROWS, (n + 1) * ROWS)
-            queries = stacked(q_ref[own, :])
-            grads = stacked(do_ref[own, :])
-            scores = dot_rows(kx[window(n), :], queries) + bias[n]
-            probs = jnp.exp(scores - lse_ref[0, n : n + 1, :])
-            grad_probs = dot_rows(vx[window(n), :], grads)
-            inner = jnp.sum(probs * grad_probs, axis=0, keepdims=True)
-            grad_scores = (probs * (grad_probs - inner)).astype(bf16)
-            dvx[window(n), :] += dot(probs.astype(bf16), grads)
-            dkx[window(n), :] += dot(grad_scores, queries)
-            outs.append(dot(turned_window(kt, kt_odd, n), grad_scores))
-        own = slice(m * PAIR, (m + 1) * PAIR)
-        grad_query = unstacked(*outs).T * 0.125
-        at = dq_at(m) * PAIR
-        dq_ref[at : at + PAIR, :] = rope_back(
-            grad_query, cos_ref[own, :], sin_ref[own, :]
-        ).astype(bf16)
+    for first in range(0, len(blocks), GROUP):
+        group = blocks[first : first + GROUP]
+        rows = [slice(n * ROWS, (n + 1) * ROWS) for n in group]
+        queries = [stacked(q_ref[own, :]) for own in rows]
+        grads = [stacked(do_ref[own, :]) for own in rows]
+        scores = [dot_rows(kx[window(n), :], query) for n, query in zip(group, queries)]
+        grad_probs = [dot_rows(vx[window(n), :], grad) for n, grad in zip(group, grads)]
+        probs = []
+        for n, score in zip(group, scores):
+            mask = bias[n]
+            mask = jnp.concatenate([mask, mask], axis=1)
+            probs.append(jnp.exp(score + mask - lse_ref[0, n : n + 1, :]))
+        inners = [jnp.sum(p * g, axis=0, keepdims=True) for p, g in zip(probs, grad_probs)]
+        grad_scores = [
+            (p * (g - inner)).astype(bf16) for p, g, inner in zip(probs, grad_probs, inners)
+        ]
+        grad_queries = [dot(kt[:, window(n)], ds) for n, ds in zip(group, grad_scores)]
+        grad_values = [dot(p.astype(bf16), grad) for p, grad in zip(probs, grads)]
+        grad_keys = [dot(ds, query) for ds, query in zip(grad_scores, queries)]
+        for n, grad_value, grad_key in zip(group, grad_values, grad_keys):
+            dvx[window(n), :] += grad_value
+            dkx[window(n), :] += grad_key
+        for n, own, grad_query in zip(group, rows, grad_queries):
+            at = dq_at(n) * ROWS
+            dq_ref[at : at + ROWS, :] = rope_back(
+                unstacked(grad_query).T * 0.125, cos_ref[own, :], sin_ref[own, :]
+            ).astype(bf16)
 
 
 def attend_back_edges_kernel(
     meta_ref, q_ref, k_ref, v_ref, do_ref, kl_ref, vl_ref, kr_ref, vr_ref, lse_ref, cos_ref, sin_ref,
     dq_ref, wk_ref, wv_ref, head_ref, tail_ref, ek_ref, ev_ref,
-    kx, vx, bias, kt, kt_odd, dkx, dvx,
+    kx, vx, bias, kt, dkx, dvx,
 ):
     rows = q_ref.shape[0]
-    blocks = rows // PAIR
-    span = PAIR + 2 * HALF
-    spans = (slice(0, span), slice(rows - PAIR, rows + 2 * HALF))
+    blocks = rows // ROWS
+    span = SPAN
+    spans = (slice(0, span), slice(rows - ROWS, rows + 2 * HALF))
 
     @pl.when(pl.program_id(0) == 0)
     def _():
-        for n in (0, 1, 2 * blocks - 2, 2 * blocks - 1):
+        for n in (0, blocks - 1):
             bias[n] = mask_bias(meta_ref, n)
 
-    fill(kx, kl_ref, k_ref, kr_ref)
-    fill(vx, vl_ref, v_ref, vr_ref)
+    inside = span - HALF
+    for x, left, own, right in ((kx, kl_ref, k_ref, kr_ref), (vx, vl_ref, v_ref, vr_ref)):
+        x[0:HALF, :] = left[...]
+        x[HALF:span, :] = own[:inside, :]
+        x[HALF + rows - inside : HALF + rows, :] = own[rows - inside :, :]
+        x[HALF + rows :, :] = right[...]
     for own in spans:
-        flip(kt, kx, own.start, own.stop, 0)
-        flip(kt_odd, kx, own.start + ROWS, own.stop, ROWS)
+        flip(kt, kx, own.start, own.stop)
         for acc in (dkx, dvx):
             acc[own, :] = jnp.zeros((span, LANES), f32)
     back_blocks(
         (0, blocks - 1), lambda n: min(n, 1),
-        q_ref, do_ref, kx, vx, bias, kt, kt_odd, lse_ref, cos_ref, sin_ref, dq_ref, dkx, dvx,
+        q_ref, do_ref, kx, vx, bias, kt, lse_ref, cos_ref, sin_ref, dq_ref, dkx, dvx,
     )
     for ref, acc in ((wk_ref, dkx), (wv_ref, dvx)):
         ref[:span, :] = acc[spans[0], :]
@@ -419,31 +423,30 @@
     meta_ref, q_ref, k_ref, v_ref, do_ref, kl_ref, vl_ref, kr_ref, vr_ref, lse_ref, cos_ref, sin_ref,
     eq_ref, wk_ref, wv_ref,
     dq_ref, dk_ref, dv_ref,
-    kx, vx, bias, kt, kt_odd, dkx, dvx,
+    kx, vx, bias, kt, dkx, dvx,
 ):
     rows = q_ref.shape[0]
-    blocks = rows // PAIR
-    span = PAIR + 2 * HALF
+    blocks = rows // ROWS
+    span = SPAN
 
     @pl.when(pl.program_id(0) == 0)
     def _():
-        for n in range(2, 2 * blocks - 2):
+        for n in range(1, blocks - 1):
             bias[n] = mask_bias(meta_ref, n)
 
     fill(kx, kl_ref, k_ref, kr_ref)
     fill(vx, vl_ref, v_ref, vr_ref)
-    flip(kt, kx, 0, kx.shape[0], 0)
-    flip(kt_odd, kx, ROWS, kx.shape[0], ROWS)
-    last = slice(rows - PAIR, rows + 2 * HALF)
+    flip(kt, kx, 0, kx.shape[0])
+    last = slice(rows - ROWS, rows + 2 * HALF)
     for acc, ref in ((dkx, wk_ref), (dvx, wv_ref)):
         acc[:span, :] = ref[:span, :]
         acc[span : last.start, :] = jnp.zeros((last.start - span, LANES), f32)
         acc[last, :] = ref[span:, :]
-    dq_ref[:PAIR, :] = eq_ref[:PAIR, :]
-    dq_ref[rows - PAIR :, :] = eq_ref[PAIR:, :]
+    dq_ref[:ROWS, :] = eq_ref[:ROWS, :]
+    dq_ref[rows - ROWS :, :] = eq_ref[ROWS:, :]
     back_blocks(
         range(1, blocks - 1), lambda n: n,
-        q_ref, do_ref, kx, vx, bias, kt, kt_odd, lse_ref, cos_ref, sin_ref, dq_ref, dkx, dvx,
+        q_ref, do_ref, kx, vx, bias, kt, lse_ref, cos_ref, sin_ref, dq_ref, dkx, dvx,
     )
     middle = slice(HALF, HALF + rows)
     dk_ref[...] = rope_back(dkx[middle, :], cos_ref[...], sin_ref[...]).astype(bf16)
@@ -519,11 +522,17 @@
     low_t = low.T
     out = mid
     dh = jnp.zeros_like(mid)
+
+    def ahead(at):
+        first, second = slice(at, at + chunk), slice(hidden + at, hidden + at + chunk)
+        products = dot(low, wm_ref[:, first]), dot(low, wm_ref[:, second])
+        return first, second, *products, dot_rows(ct, wd_ref[first, :])
+
+    begun = ahead(0)
     for at in range(0, hidden, chunk):
-        first, second = slice(at, at + chunk), slice(hidden + at, hidden + at + chunk)
-        a1 = dot(low, wm_ref[:, first])
-        a2 = dot(low, wm_ref[:, second])
-        du = dot_rows(ct, wd_ref[first, :])
+        first, second, a1, a2, du = begun
+        if at + chunk < hidden:
+            begun = ahead(at + chunk)
         phi = 0.5 * (1.0 + lax.erf(a1 * (1.0 / math.sqrt(2.0))))
         gate = a1 * phi
         u = (gate * a2).astype(bf16)
@@ -703,9 +712,8 @@
     return [
         pltpu.VMEM((extended, LANES), bf16),
         pltpu.VMEM((extended, LANES), bf16),
-        pltpu.VMEM((rows // ROWS, SPAN, LANES), f32),
+        pltpu.VMEM((rows // ROWS, SPAN, ROWS), f32),
         pltpu.VMEM((LANES, extended), bf16),
-        pltpu.VMEM((LANES, extended - ROWS), bf16),
     ]
 
 
@@ -725,9 +733,9 @@
         + [pl.BlockSpec(memory_space=pl.ANY)] * len(before),
         [
             pl.BlockSpec((LANES, rows), lambda i: (i + first, 0)),
-            pl.BlockSpec((1, rows // ROWS, LANES), lambda i: (i + first, 0, 0)),
+            pl.BlockSpec((1, rows // ROWS, 2 * ROWS), lambda i: (i + first, 0, 0)),
         ],
-        [shaped((width, rows), bf16), shaped((steps, rows // ROWS, LANES), f32)],
+        [shaped((width, rows), bf16), shaped((steps, rows // ROWS, 2 * ROWS), f32)],
         attend_scratch(rows),
         8 * rows * width * 256,
         rows * width * 8,
@@ -740,7 +748,7 @@
         [pl.BlockSpec(memory_space=pltpu.SMEM)]
         + [pairs(rows)] * 4
         + [pairs(HALF), pairs(HALF, steps)] * 2
-        + [pl.BlockSpec((1, rows // ROWS, LANES), lambda i: (i, 0, 0)), held(rows, LANES), held(rows, LANES)]
+        + [pl.BlockSpec((1, rows // ROWS, 2 * ROWS), lambda i: (i, 0, 0)), held(rows, LANES), held(rows, LANES)]
     )
 
 
@@ -752,21 +760,21 @@
 def attend_back_edges(meta, q, k, v, do, left, right, lse, cos, sin):
     rows, width = q.shape
     steps = width // LANES
-    span = 2 * (PAIR + 2 * HALF)
+    span = 2 * SPAN
     return call(
         attend_back_edges_kernel,
         steps,
         back_specs(rows, steps),
-        [pairs(2 * PAIR)]
+        [pairs(2 * ROWS)]
         + [pairs(span)] * 2
         + [pl.BlockSpec((2, HALF, LANES), lambda i: (0, 0, i))] * 2
         + [pairs(2 * HALF)] * 2,
-        [shaped((2 * PAIR, width), bf16)]
+        [shaped((2 * ROWS, width), bf16)]
         + [shaped((span, width), f32)] * 2
         + [shaped((2, HALF, width), bf16)] * 2
         + [shaped((2 * HALF, width), f32)] * 2,
         back_scratch(rows),
-        20 * 2 * PAIR * width * 256,
+        20 * 2 * ROWS * width * 256,
         rows * width * 10,
     )(meta, q, k, v, do, left, left, right, right, lse, cos, sin)
 
@@ -774,11 +782,11 @@
 def attend_back(meta, q, k, v, do, left, right, lse, cos, sin, edges):
     rows, width = q.shape
     steps = width // LANES
-    span = 2 * (PAIR + 2 * HALF)
+    span = 2 * SPAN
     return call(
         attend_back_kernel,
         steps,
-        back_specs(rows, steps) + [pairs(2 * PAIR)] + [pairs(span)] * 2,
+        back_specs(rows, steps) + [pairs(2 * ROWS)] + [pairs(span)] * 2,
         [pairs(rows)] * 3,
         [shaped((rows, width), bf16)] * 3,
         back_scratch(rows),
@@ -817,7 +825,7 @@
 
 def qkv_gradient(split, place, h, dq, dk, dv, ek, ev, left, right, cos, sin):
     rows, width = h.shape
-    tile = WIDE_TILE if rows % WIDE_TILE == 0 else rows
+    tile = min(TILE, rows)
     grads = [(width, 3 * width // 2)] * 2 if split else [(width, 3 * width)]
     return call(
         functools.partial(qkv_grad_kernel, split),
@@ -906,6 +914,9 @@
     low = jnp.where(device > 0, -HALF, 0)
     high = jnp.where(device < last_device, rows + HALF, rows)
     meta = jnp.stack([start, low, high]).astype(jnp.int32)
+    edge_x, edge_cos, edge_sin = (
+        jnp.concatenate(edge_rows(value), axis=0) for value in (tokens, cos, sin)
+    )
     shards = lax.axis_size("shard")
     quarters = lax.axis_size("seq") // 2
     core = lax.axis_index("seq") % 2
@@ -938,7 +949,7 @@
         )
         qkv_part = jnp.concatenate([piece[:slot] for piece in qkv_stack], axis=0)
         qkv_part = jnp.concatenate(stack(qkv_part, "seq", 2), axis=0)
-        qkv_part = after(qkv_part, rest_part)
+        qkv_part = after(qkv_part, rest_part, gains, meta, place, edge_x, edge_cos, edge_sin)
         rest_part = after(rest_part, qkv_part)
         qkv_parts = qkv_part, swap(qkv_part, "seq", 1)
     else:
@@ -947,9 +958,6 @@
         )
         gains = lax.all_gather(norm_gains.astype(bf16), "shard", axis=1, tiled=True).astype(f32)
         qkv_parts = (full_qkv,)
-    edge_x, edge_cos, edge_sin = (
-        jnp.concatenate(edge_rows(value), axis=0) for value in (tokens, cos, sin)
-    )
     kv_head, kv_tail, full_qkv = project_edges(
         split, place, edge_x, gains, edge_cos, edge_sin, *qkv_parts
     )

time: 329 us -> 312 us (0.948)
  Pallas kernels: 171 us -> 144 us
  waiting for transfers between devices: 34.1 us -> 39.8 us
  local copies, waits for them, and re-layouts: 28.7 us -> 33.9 us
  starting transfers between devices: 59.9 us -> 56.1 us
    pallas_call x2, Pallas kernels: 33.9 us -> 18 us  [attend(): call(attend_kernel, count, [pl.BlockSpec(memory_space=pltpu.SMEM)] + [col...]
    pallas_call x1, Pallas kernels: 28.2 us -> 19.5 us  [attend_back(): call(attend_back_kernel, steps, back_specs(rows, steps) + [pairs(2 * ROWS...]
    ppermute x36, waiting for transfers between devices: 34.1 us -> 39.8 us  [swap(): return lax.ppermute(value, axis, [(i, i ^ flip) for i in range(count)])]
    ppermute x36, starting transfers between devices: 47.2 us -> 43.4 us  [swap(): return lax.ppermute(value, axis, [(i, i ^ flip) for i in range(count)])]
    unnamed x66 -> x68, local copies, waits for them, and re-layouts: 12.4 us -> 15.6 us
  transfers between devices with their start and end apart: 40 -> 40, of which waited for: 9 -> 16; matrix products, arithmetic and copies ran while one was open for 10% -> 13% of each run, Pallas kernels for 34% -> 27%
where the time goes in v1:
time: 312 us
  Pallas kernels  144 us (46%)
  starting transfers between devices  56.1 us (18%)
  waiting for transfers between devices  39.8 us (13%)
  other arithmetic  36.9 us (12%)
  local copies, waits for them, and re-layouts  33.9 us (11%)
    pallas_call x1, Pallas kernels, middle(): call(functools.partial(middle_kernel, split), rows // tile, [pl.BlockSpec...  59.4 us
    ppermute x36, starting transfers between devices, swap(): return lax.ppermute(value, axis, [(i, i ^ flip) for i in range(count)])  43.4 us
    ppermute x36, waiting for transfers between devices, swap(): return lax.ppermute(value, axis, [(i, i ^ flip) for i in range(count)])  39.8 us
    pallas_call x1, Pallas kernels, attend_back(): call(attend_back_kernel, steps, back_specs(rows, steps) + [pairs(2 * ROWS...  19.5 us
    pallas_call x2, Pallas kernels, attend(): call(attend_kernel, count, [pl.BlockSpec(memory_space=pltpu.SMEM)] + [col...  18 us
    unnamed x68, local copies, waits for them, and re-layouts  15.6 us
    pallas_call x1, Pallas kernels, input_gradient(): call(input_kernel, rows // tile, [tiles(tile, width), held(2, width), kep...  11.2 us
    pallas_call x1, Pallas kernels, qkv_gradient(): call(functools.partial(qkv_grad_kernel, split), rows // tile, [pl.BlockSp...  11.1 us
  transfers between devices with their start and end apart: 40, of which 16 were waited for; matrix products, arithmetic and copies ran while one was open for 13% of the time, Pallas kernels for 27%

profile of v1, /device:TPU:0, one launch (start us, length us, event | category | flops | bytes accessed | tf_op | source)
XLA Modules:
  0.0 312.2 jit_solution(3684395625520098168)
XLA Ops:
  0.7 2.6 convert_element_type.150
  5.7 3.0 collective-permute-start
  8.7 2.6 collective-permute-start.1
  21.0 3.0 fusion.14
  30.1 3.5 %collective-permute-start.7 = (bf16[48,2304]{1,0:T(8,128)(2,1)S(1)}, bf16[48,2304]{1,0:T(8,128)(2,1)}, u32[]{:S(2)}, u32[]{:S(2)}) collective-permute-start(bf16[48,2304]{1,0:T(8,128)(2,1)S(1)} %pad_maximum_fusion.6), channel_id=1, source_target_pairs={{0,2},{1,3},{2,0},{3,1},{4,6},{5,7},{6,4},{7,5},{8,10},{9,11},{10,... | collective-permute-start | bytes 663560 | tf_op jit(solution)/shard_map/ppermute | solution.py:39
  43.6 6.0 %collective-permute-done.7 = bf16[48,2304]{1,0:T(8,128)(2,1)} collective-permute-done((bf16[48,2304]{1,0:T(8,128)(2,1)S(1)}, bf16[48,2304]{1,0:T(8,128)(2,1)}, u32[]{:S(2)}, u32[]{:S(2)}) %collective-permute-start.7) | collective-permute-done | bytes 221216 | tf_op jit(solution)/shard_map/ppermute | solution.py:39
  49.5 2.1 pad_maximum_fusion
  51.7 7.0 %collective-permute-done.4 = bf16[192,1152]{1,0:T(8,128)(2,1)} collective-permute-done((bf16[192,1152]{1,0:T(8,128)(2,1)}, bf16[192,1152]{1,0:T(8,128)(2,1)}, u32[]{:S(2)}, u32[]{:S(2)}) %collective-permute-start.4) | collective-permute-done | bytes 442400 | tf_op jit(solution)/shard_map/ppermute | solution.py:39
  65.9 5.1 %shard_map.305 = (bf16[64,1536]{1,0:T(8,128)(2,1)}, bf16[64,1536]{1,0:T(8,128)(2,1)}, bf16[768,2304]{1,0:T(8,128)(2,1)}) custom-call(s32[3]{0:T(128)} %get-tuple-element.206.place_ref, bf16[128,768]{1,0:T(8,128)(2,1)} %pad_maximum_fusion.9.x_ref, f32[2,768]{1,0:T(2,128)} %reshape.111.gain_ref, f32[128,128]{1,0:T(8,128)} %pad_maximum_fusion.10.cos_ref, ...), custom_call_target="tpu_custom_call" | custom-call | flops 4718592 | bytes 119808 | tf_op jit(solution)/shard_map/pallas_call | solution.py:696
  72.2 4.9 %collective-permute-start.11 = (bf16[64,1536]{1,0:T(8,128)(2,1)}, bf16[64,1536]{1,0:T(8,128)(2,1)S(1)}, u32[]{:S(2)}, u32[]{:S(2)}) collective-permute-start(bf16[64,1536]{1,0:T(8,128)(2,1)} %get-tuple-element.92), channel_id=1, source_target_pairs={{0,1},{1,2},{2,3},{3,4},{4,5},{5,6},{6,7},{7,8},{8,9},{9,10},{10,1... | collective-permute-start | bytes 589832 | tf_op jit(solution)/shard_map/ppermute | solution.py:164
  78.4 10.1 %shard_map.306 = (bf16[1280,768]{1,0:T(8,128)(2,1)}, bf16[1280,768]{1,0:T(8,128)(2,1)}, bf16[1280,768]{1,0:T(8,128)(2,1)}, bf16[1280,768]{1,0:T(8,128)(2,1)}) custom-call(bf16[1280,768]{1,0:T(8,128)(2,1)} %x_ref.4, f32[2,768]{1,0:T(2,128)} %reshape.111.gain_ref, bf16[768,2304]{1,0:T(8,128)(2,1)} %get-tuple-element.87.w_ref, f32[1280,128]{1,0:T(8,128)} %copy-done.3, ...), custom_call_target="tpu_custom_call" | custom-call | flops 70778880 | bytes 208896 | tf_op jit(solution)/shard_map/pallas_call | solution.py:682
  89.3 8.5 %shard_map.307 = (bf16[768,1280]{1,0:T(8,128)(2,1)}, f32[6,10,256]{2,1,0:T(8,128)}) custom-call(s32[3]{0:T(128)} %get-tuple-element.207.meta_ref, bf16[1280,768]{1,0:T(8,128)(2,1)} %get-tuple-element.99.q_ref, bf16[1280,768]{1,0:T(8,128)(2,1)} %get-tuple-element.90.k_ref, bf16[1280,768]{1,0:T(8,128)(2,1)} %get-tuple-element.91.v_ref, ...), custom_call_target="tpu_custom_call" | custom-call | flops 31457280 | bytes 122880 | tf_op jit(solution)/shard_map/pallas_call | solution.py:727
  97.8 5.6 %collective-permute-done.13 = bf16[192,2304]{1,0:T(8,128)(2,1)} collective-permute-done((bf16[192,2304]{1,0:T(8,128)(2,1)}, bf16[192,2304]{1,0:T(8,128)(2,1)}, u32[]{:S(2)}, u32[]{:S(2)}) %collective-permute-start.13) | collective-permute-done | bytes 884768 | tf_op jit(solution)/shard_map/ppermute | solution.py:39
  109.2 9.5 %shard_map.308 = (bf16[768,1280]{1,0:T(8,128)(2,1)}, f32[6,10,256]{2,1,0:T(8,128)}) custom-call(s32[3]{0:T(128)} %get-tuple-element.207.meta_ref, bf16[1280,768]{1,0:T(8,128)(2,1)} %get-tuple-element.99.q_ref, bf16[1280,768]{1,0:T(8,128)(2,1)} %get-tuple-element.90.k_ref, ...), custom_call_target="tpu_custom_call", output_to_operand_aliasing={{0}: (8, {}), {1}: (9, {})} | custom-call | flops 31457280 | bytes 122880 | tf_op jit(solution)/shard_map/pallas_call | solution.py:727
  118.6 59.4 %shard_map.309 = (bf16[1280,768]{1,0:T(8,128)(2,1)}, bf16[1280,768]{1,0:T(8,128)(2,1)}, bf16[1280,768]{1,0:T(8,128)(2,1)}, bf16[768,2304]{1,0:T(8,128)(2,1)}, bf16[768,2304]{1,0:T(8,128)(2,1)}) custom-call(s32[3]{0:T(128)} %get-tuple-element.206.place_ref, bf16[1280,768]{1,0:T(8,128)(2,1)} %x_ref.4, bf16[768,1280]{1,0:T(8,128)(2,1)} %get-tuple-element.101.o_ref, ...), custom_call_target="tpu_custom_call" | custom-call | flops 353894400 | bytes 399360 | tf_op jit(solution)/shard_map/pallas_call | solution.py:806
  178.1 9.5 %shard_map.310 = (bf16[256,768]{1,0:T(8,128)(2,1)}, f32[512,768]{1,0:T(8,128)}, f32[512,768]{1,0:T(8,128)}, bf16[2,64,768]{2,1,0:T(8,128)(2,1)}, bf16[2,64,768]{...) custom-call(s32[3]{0:T(128)} %get-tuple-element.207.meta_ref, bf16[1280,768]{1,0:T(8,128)(2,1)} %get-tuple-element.99.q_ref, ...), custom_call_target="tpu_custom_call" | custom-call | flops 15728640 | bytes 153600 | tf_op jit(solution)/shard_map/pallas_call | solution.py:764
  189.5 3.9 %add_convert_fusion = bf16[768,2304]{1,0:T(8,128)(2,1)S(1)} fusion(bf16[768,2304]{1,0:T(8,128)(2,1)} %copy-done.9, bf16[768,2304]{1,0:T(8,128)(2,1)} %get-tuple-element.105), kind=kLoop, calls=%fused_computation | loop fusion | flops 7077888 | bytes 10616832 | tf_op jit(solution)/shard_map/convert_element_type | solution.py:118
  195.8 2.6 collective-permute-start.21
  199.7 5.2 %collective-permute-start.17 = (bf16[2,64,768]{2,1,0:T(8,128)(2,1)}, bf16[2,64,768]{2,1,0:T(8,128)(2,1)}, u32[]{:S(2)}, u32[]{:S(2)}) collective-permute-start(bf16[2,64,768]{2,1,0:T(8,128)(2,1)} %get-tuple-element.120), channel_id=1, source_target_pairs={{0,1},{1,2},{2,3},{3,4},{4,5},{5,6},{6,7},{7,8},{8,9},{9,10},{10,1... | collective-permute-start | bytes 589832 | tf_op jit(solution)/shard_map/ppermute | solution.py:164
  204.9 19.5 %shard_map.311 = (bf16[1280,768]{1,0:T(8,128)(2,1)}, bf16[1280,768]{1,0:T(8,128)(2,1)}, bf16[1280,768]{1,0:T(8,128)(2,1)}) custom-call(s32[3]{0:T(128)} %get-tuple-element.207.meta_ref, bf16[1280,768]{1,0:T(8,128)(2,1)} %get-tuple-element.99.q_ref, bf16[1280,768]{1,0:T(8,128)(2,1)} %get-tuple-element.90.k_ref, bf16[1280,768]{1,0:T(8,128)(2,1)} %get-tuple-element.91.v_ref, ...), custom_call_target="tpu_custom_call" | custom-call | flops 78643200 | bytes 215040 | tf_op jit(solution)/shard_map/pallas_call | solution.py:786
  224.5 11.1 %shard_map.312 = (bf16[128,768]{1,0:T(8,128)(2,1)}, bf16[128,768]{1,0:T(8,128)(2,1)}, bf16[768,1152]{1,0:T(8,128)(2,1)}, bf16[768,1152]{1,0:T(8,128)(2,1)}) custom-call(s32[3]{0:T(128)} %get-tuple-element.206.place_ref, bf16[1280,768]{1,0:T(8,128)(2,1)} %get-tuple-element.115.h_ref, bf16[1280,768]{1,0:T(8,128)(2,1)} %get-tuple-element.129.dq_ref, ...), custom_call_target="tpu_custom_call" | custom-call | flops 70778880 | bytes 178176 | tf_op jit(solution)/shard_map/pallas_call | solution.py:830
  236.5 3.2 %fusion.8 = bf16[4,48,2304]{2,1,0:T(8,128)(2,1)} fusion(bf16[4,48,2304]{2,1,0:T(8,128)(2,1)} %collective-permute-done.21, bf16[4,48,2304]{2,1,0:T(8,128)(2,1)} %collective-permute-done.20, bf16[4,48,2304]{2,1,0:T(8,128)(2,1)} %collective-permute-done.19, bf16[4,4,48,2304]{3,2,1,0:T(8,128)(2,1)S(1)} %bitcast.93, s32[]{:T(128)S(6)} %select_n.165), kind=kLoop, calls=%fused_computation.19 | loop fusion | flops 3538944 | bytes 4423684 | tf_op jit(solution)/shard_map/convert_element_type | solution.py:118
  239.8 3.5 %collective-permute-done.22 = bf16[768,1152]{1,0:T(8,128)(2,1)S(1)} collective-permute-done((bf16[768,1152]{1,0:T(8,128)(2,1)S(1)}, bf16[768,1152]{1,0:T(8,128)(2,1)S(1)}, u32[]{:S(2)}, u32[]{:S(2)}) %collective-permute-start.22) | collective-permute-done | bytes 1769504 | tf_op jit(solution)/shard_map/ppermute | solution.py:39
  250.4 4.6 %collective-permute-start.28 = (bf16[48,2304]{1,0:T(8,128)(2,1)}, bf16[48,2304]{1,0:T(8,128)(2,1)S(1)}, u32[]{:S(2)}, u32[]{:S(2)}) collective-permute-start(bf16[48,2304]{1,0:T(8,128)(2,1)} %get-tuple-element.186), channel_id=1, source_target_pairs={{0,2},{1,3},{2,0},{3,1},{4,6},{5,7},{6,4},{7,5},{8,10},{9,11},{10,... | collective-permute-start | bytes 663560 | tf_op jit(solution)/shard_map/ppermute | solution.py:39
  255.0 11.2 %shard_map.313 = bf16[1280,768]{1,0:T(8,128)(2,1)} custom-call(bf16[1280,768]{1,0:T(8,128)(2,1)} %x_ref.4, f32[2,768]{1,0:T(2,128)} %reshape.111.gain_ref, bf16[768,2304]{1,0:T(8,128)(2,1)} %get-tuple-element.87.w_ref, bf16[1280,768]{1,0:T(8,128)(2,1)} %get-tuple-element.103.dmid_ref, bf16[1280,768]{1,0:T(8,128)(2,1)} %get-tuple-element.129.dq_ref, ...), custom_call_target="tpu_custom_call" | custom-call | flops 70778880 | bytes 270336 | tf_op jit(solution)/shard_map/pallas_call | solution.py:849
  270.8 3.7 %collective-permute-done.29 = bf16[48,2304]{1,0:T(8,128)(2,1)S(1)} collective-permute-done((bf16[48,2304]{1,0:T(8,128)(2,1)}, bf16[48,2304]{1,0:T(8,128)(2,1)S(1)}, u32[]{:S(2)}, u32[]{:S(2)}) %collective-permute-start.29) | collective-permute-done | bytes 221216 | tf_op jit(solution)/shard_map/ppermute | solution.py:39
  274.6 3.1 collective-permute-start.26
  277.7 2.4 collective-permute-start.31
  283.8 3.5 %collective-permute-done.30 = bf16[48,1152]{1,0:T(8,128)(2,1)S(1)} collective-permute-done((bf16[48,1152]{1,0:T(8,128)(2,1)S(1)}, bf16[48,1152]{1,0:T(8,128)(2,1)S(1)}, u32[]{:S(2)}, u32[]{:S(2)}) %collective-permute-start.30) | collective-permute-done | bytes 110624 | tf_op jit(solution)/shard_map/ppermute | solution.py:39
  298.6 3.4 %multiply_subtract_fusion = (f32[192,2304]{1,0:T(8,128)}, f32[192,2304]{1,0:T(8,128)}, f32[192,2304]{1,0:T(8,128)}, f32[192]{0:T(256)S(1)}) fusion(f32[192,2304]{1,0:T(8,128)S(1)} %copy-done.5, bf16[192,1152]{1,0:T(8,128)(2,1)S(1)} %slice.122, bf16[192,1152]{1,0:T(8,128)(2,1)S(1)} %slice.121, f32[192,2304]{1,0:T(8,128)S(1)} %copy-done.13, ...), kind=kLoop, calls=%fused_computation.20 | loop fusion | flops 10174272 | bytes 11502336 | tf_op jit(solution)/shard_map/sub | solution.py:879
  304.4 2.0 multiply_subtract_fusion.2
  308.0 3.4 %multiply_subtract_fusion.1 = (f32[192,2304]{1,0:T(8,128)}, f32[192,2304]{1,0:T(8,128)}, f32[192,2304]{1,0:T(8,128)}, f32[192]{0:T(256)S(1)}) fusion(f32[192,2304]{1,0:T(8,128)S(1)} %copy-done.6, bf16[192,1152]{1,0:T(8,128)(2,1)S(1)} %get-tuple-element.183, bf16[192,1152]{1,0:T(8,128)(2,1)S(1)} %get-tuple-element.182, f32[192,2304]{1,0:T(8,128)S(1)} %copy-done.15, ...), kind=kLoop, calls=%fused_computation.21 | loop fusion | flops 10174272 | bytes 11502336 | tf_op jit(solution)/shard_map/sub | solution.py:879
  (208 shorter events, 81.5 us)
Async XLA Ops:
  5.7 23.6 %collective-permute-start = (bf16[56,1152]{1,0:T(8,128)(2,1)}, bf16[56,1152]{1,0:T(8,128)(2,1)}, u32[]{:S(2)}, u32[]{:S(2)}) collective-permute-start(bf16[56,1152]{1,0:T(8,128)(2,1)} %fusion.24), channel_id=1, source_target_pairs={{0,1},{1,0},{2,3},{3,2},{4,5},{5,4},{6,7},{7,6},{8,9},{9,8},{10,11... | collective-permute-start | bytes 387080 | tf_op jit(solution)/shard_map/ppermute | solution.py:39
  8.7 25.8 %collective-permute-start.1 = (bf16[56,1152]{1,0:T(8,128)(2,1)}, bf16[56,1152]{1,0:T(8,128)(2,1)}, u32[]{:S(2)}, u32[]{:S(2)}) collective-permute-start(bf16[56,1152]{1,0:T(8,128)(2,1)} %fusion.24), channel_id=1, source_target_pairs={{0,2},{1,3},{2,0},{3,1},{4,6},{5,7},{6,4},{7,5},{8,10},{9,11},{10,... | collective-permute-start | bytes 387080 | tf_op jit(solution)/shard_map/ppermute | solution.py:39
  11.3 24.2 %collective-permute-start.2 = (bf16[56,1152]{1,0:T(8,128)(2,1)}, bf16[56,1152]{1,0:T(8,128)(2,1)}, u32[]{:S(2)}, u32[]{:S(2)}) collective-permute-start(bf16[56,1152]{1,0:T(8,128)(2,1)} %fusion.24), channel_id=1, source_target_pairs={{0,3},{1,2},{2,1},{3,0},{4,7},{5,6},{6,5},{7,4},{8,11},{9,10},{10,... | collective-permute-start | bytes 387080 | tf_op jit(solution)/shard_map/ppermute | solution.py:39
  29.2 14.1 %collective-permute-start.6 = (bf16[48,2304]{1,0:T(8,128)(2,1)S(1)}, bf16[48,2304]{1,0:T(8,128)(2,1)}, u32[]{:S(2)}, u32[]{:S(2)}) collective-permute-start(bf16[48,2304]{1,0:T(8,128)(2,1)S(1)} %pad_maximum_fusion.6), channel_id=1, source_target_pairs={{0,1},{1,0},{2,3},{3,2},{4,5},{5,4},{6,7},{7,6},{8,9},{9,8},{10,11... | collective-permute-start | bytes 663560 | tf_op jit(solution)/shard_map/ppermute | solution.py:39
  30.1 19.4 %collective-permute-start.7 = (bf16[48,2304]{1,0:T(8,128)(2,1)S(1)}, bf16[48,2304]{1,0:T(8,128)(2,1)}, u32[]{:S(2)}, u32[]{:S(2)}) collective-permute-start(bf16[48,2304]{1,0:T(8,128)(2,1)S(1)} %pad_maximum_fusion.6), channel_id=1, source_target_pairs={{0,2},{1,3},{2,0},{3,1},{4,6},{5,7},{6,4},{7,5},{8,10},{9,11},{10,... | collective-permute-start | bytes 663560 | tf_op jit(solution)/shard_map/ppermute | solution.py:39
  33.6 15.9 %collective-permute-start.8 = (bf16[48,2304]{1,0:T(8,128)(2,1)S(1)}, bf16[48,2304]{1,0:T(8,128)(2,1)}, u32[]{:S(2)}, u32[]{:S(2)}) collective-permute-start(bf16[48,2304]{1,0:T(8,128)(2,1)S(1)} %pad_maximum_fusion.6), channel_id=1, source_target_pairs={{0,3},{1,2},{2,1},{3,0},{4,7},{5,6},{6,5},{7,4},{8,11},{9,10},{10,... | collective-permute-start | bytes 663560 | tf_op jit(solution)/shard_map/ppermute | solution.py:39
  37.2 14.5 %collective-permute-start.3 = (bf16[192,1152]{1,0:T(8,128)(2,1)}, bf16[192,1152]{1,0:T(8,128)(2,1)}, u32[]{:S(2)}, u32[]{:S(2)}) collective-permute-start(bf16[192,1152]{1,0:T(8,128)(2,1)} %pad_maximum_fusion.3), channel_id=1, source_target_pairs={{0,8},{4,12},{8,0},{12,4},{16,24},{20,28},{24,16},{28,20},{1,9},{5... | collective-permute-start | bytes 1327112 | tf_op jit(solution)/shard_map/ppermute | solution.py:39
  38.9 19.8 %collective-permute-start.4 = (bf16[192,1152]{1,0:T(8,128)(2,1)}, bf16[192,1152]{1,0:T(8,128)(2,1)}, u32[]{:S(2)}, u32[]{:S(2)}) collective-permute-start(bf16[192,1152]{1,0:T(8,128)(2,1)} %pad_maximum_fusion.3), channel_id=1, source_target_pairs={{0,16},{4,20},{8,24},{12,28},{16,0},{20,4},{24,8},{28,12},{1,17},{... | collective-permute-start | bytes 1327112 | tf_op jit(solution)/shard_map/ppermute | solution.py:39
  43.3 17.6 %collective-permute-start.5 = (bf16[192,1152]{1,0:T(8,128)(2,1)}, bf16[192,1152]{1,0:T(8,128)(2,1)S(1)}, u32[]{:S(2)}, u32[]{:S(2)}) collective-permute-start(bf16[192,1152]{1,0:T(8,128)(2,1)} %pad_maximum_fusion.3), channel_id=1, source_target_pairs={{0,24},{4,28},{8,16},{12,20},{16,8},{20,12},{24,0},{28,4},{1,25},{... | collective-permute-start | bytes 1327112 | tf_op jit(solution)/shard_map/ppermute | solution.py:39
  61.0 36.9 %collective-permute-start.14 = (bf16[192,2304]{1,0:T(8,128)(2,1)}, bf16[192,2304]{1,0:T(8,128)(2,1)}, u32[]{:S(2)}, u32[]{:S(2)}) collective-permute-start(bf16[192,2304]{1,0:T(8,128)(2,1)} %pad_maximum_fusion), channel_id=1, source_target_pairs={{0,24},{4,28},{8,16},{12,20},{16,8},{20,12},{24,0},{28,4},{1,25},{... | collective-permute-start | bytes 2654216 | tf_op jit(solution)/shard_map/ppermute | solution.py:39
  62.5 40.9 %collective-permute-start.13 = (bf16[192,2304]{1,0:T(8,128)(2,1)}, bf16[192,2304]{1,0:T(8,128)(2,1)}, u32[]{:S(2)}, u32[]{:S(2)}) collective-permute-start(bf16[192,2304]{1,0:T(8,128)(2,1)} %pad_maximum_fusion), channel_id=1, source_target_pairs={{0,16},{4,20},{8,24},{12,28},{16,0},{20,4},{24,8},{28,12},{1,17},{... | collective-permute-start | bytes 2654216 | tf_op jit(solution)/shard_map/ppermute | solution.py:39
  62.6 42.8 %collective-permute-start.10 = (bf16[192,2304]{1,0:T(8,128)(2,1)}, bf16[192,2304]{1,0:T(8,128)(2,1)}, u32[]{:S(2)}, u32[]{:S(2)}) collective-permute-start(bf16[192,2304]{1,0:T(8,128)(2,1)} %pad_maximum_fusion), channel_id=1, source_target_pairs={{0,8},{4,12},{8,0},{12,4},{16,24},{20,28},{24,16},{28,20},{1,9},{5... | collective-permute-start | bytes 2654216 | tf_op jit(solution)/shard_map/ppermute | solution.py:39
  70.9 17.6 %collective-permute-start.12 = (bf16[64,1536]{1,0:T(8,128)(2,1)}, bf16[64,1536]{1,0:T(8,128)(2,1)S(1)}, u32[]{:S(2)}, u32[]{:S(2)}) collective-permute-start(bf16[64,1536]{1,0:T(8,128)(2,1)} %get-tuple-element.85), channel_id=1, source_target_pairs={{1,0},{2,1},{3,2},{4,3},{5,4},{6,5},{7,6},{8,7},{9,8},{10,9},{11,1... | collective-permute-start | bytes 589832 | tf_op jit(solution)/shard_map/ppermute | solution.py:170
  72.2 16.3 %collective-permute-start.11 = (bf16[64,1536]{1,0:T(8,128)(2,1)}, bf16[64,1536]{1,0:T(8,128)(2,1)S(1)}, u32[]{:S(2)}, u32[]{:S(2)}) collective-permute-start(bf16[64,1536]{1,0:T(8,128)(2,1)} %get-tuple-element.92), channel_id=1, source_target_pairs={{0,1},{1,2},{2,3},{3,4},{4,5},{5,6},{6,7},{7,8},{8,9},{9,10},{10,1... | collective-permute-start | bytes 589832 | tf_op jit(solution)/shard_map/ppermute | solution.py:164
  109.1 9.5 %collective-permute-start.15 = (bf16[768,2304]{1,0:T(8,128)(2,1)S(1)}, bf16[768,2304]{1,0:T(8,128)(2,1)}, u32[]{:S(2)}, u32[]{:S(2)}) collective-permute-start(bf16[768,2304]{1,0:T(8,128)(2,1)S(1)} %constant_dynamic-update-slice_fusion.7.refs_0_), channel_id=1, source_target_pairs={{0,4},{4,0},{8,12},{12,8},{16,20},{20,16},{24,28},{28,24},{1,5},{5... | collective-permute-start | bytes 10616840 | tf_op jit(solution)/shard_map/ppermute | solution.py:39
  178.1 9.6 %collective-permute-start.16 = (bf16[768,2304]{1,0:T(8,128)(2,1)}, bf16[768,2304]{1,0:T(8,128)(2,1)S(1)}, u32[]{:S(2)}, u32[]{:S(2)}) collective-permute-start(bf16[768,2304]{1,0:T(8,128)(2,1)} %get-tuple-element.106), channel_id=1, source_target_pairs={{0,4},{4,0},{8,12},{12,8},{16,20},{20,16},{24,28},{28,24},{1,5},{5... | collective-permute-start | bytes 10616840 | tf_op jit(solution)/shard_map/ppermute | solution.py:39
  194.9 40.6 %collective-permute-start.19 = (bf16[4,48,2304]{2,1,0:T(8,128)(2,1)}, bf16[4,48,2304]{2,1,0:T(8,128)(2,1)}, u32[]{:S(2)}, u32[]{:S(2)}) collective-permute-start(bf16[4,48,2304]{2,1,0:T(8,128)(2,1)} %get-tuple-element.170), channel_id=1, source_target_pairs={{0,8},{4,12},{8,0},{12,4},{16,24},{20,28},{24,16},{28,20},{1,9},{5... | collective-permute-start | bytes 2654216 | tf_op jit(solution)/shard_map/ppermute | solution.py:39
  195.5 41.0 %collective-permute-start.20 = (bf16[4,48,2304]{2,1,0:T(8,128)(2,1)}, bf16[4,48,2304]{2,1,0:T(8,128)(2,1)}, u32[]{:S(2)}, u32[]{:S(2)}) collective-permute-start(bf16[4,48,2304]{2,1,0:T(8,128)(2,1)} %get-tuple-element.172), channel_id=1, source_target_pairs={{0,16},{4,20},{8,24},{12,28},{16,0},{20,4},{24,8},{28,12},{1,17},{... | collective-permute-start | bytes 2654216 | tf_op jit(solution)/shard_map/ppermute | solution.py:39
  195.8 40.7 %collective-permute-start.21 = (bf16[4,48,2304]{2,1,0:T(8,128)(2,1)}, bf16[4,48,2304]{2,1,0:T(8,128)(2,1)}, u32[]{:S(2)}, u32[]{:S(2)}) collective-permute-start(bf16[4,48,2304]{2,1,0:T(8,128)(2,1)} %get-tuple-element.171), channel_id=1, source_target_pairs={{0,24},{4,28},{8,16},{12,20},{16,8},{20,12},{24,0},{28,4},{1,25},{... | collective-permute-start | bytes 2654216 | tf_op jit(solution)/shard_map/ppermute | solution.py:39
  198.4 26.0 %collective-permute-start.18 = (bf16[2,64,768]{2,1,0:T(8,128)(2,1)}, bf16[2,64,768]{2,1,0:T(8,128)(2,1)}, u32[]{:S(2)}, u32[]{:S(2)}) collective-permute-start(bf16[2,64,768]{2,1,0:T(8,128)(2,1)} %get-tuple-element.108), channel_id=1, source_target_pairs={{1,0},{2,1},{3,2},{4,3},{5,4},{6,5},{7,6},{8,7},{9,8},{10,9},{11,1... | collective-permute-start | bytes 589832 | tf_op jit(solution)/shard_map/ppermute | solution.py:170
  199.7 24.7 %collective-permute-start.17 = (bf16[2,64,768]{2,1,0:T(8,128)(2,1)}, bf16[2,64,768]{2,1,0:T(8,128)(2,1)}, u32[]{:S(2)}, u32[]{:S(2)}) collective-permute-start(bf16[2,64,768]{2,1,0:T(8,128)(2,1)} %get-tuple-element.120), channel_id=1, source_target_pairs={{0,1},{1,2},{2,3},{3,4},{4,5},{5,6},{6,7},{7,8},{8,9},{9,10},{10,1... | collective-permute-start | bytes 589832 | tf_op jit(solution)/shard_map/ppermute | solution.py:164
  244.9 21.3 %collective-permute-start.23 = (bf16[4,48,1152]{2,1,0:T(8,128)(2,1)}, bf16[4,48,1152]{2,1,0:T(8,128)(2,1)S(1)}, u32[]{:S(2)}, u32[]{:S(2)}) collective-permute-start(bf16[4,48,1152]{2,1,0:T(8,128)(2,1)} %get-tuple-element.177), channel_id=1, source_target_pairs={{0,8},{4,12},{8,0},{12,4},{16,24},{20,28},{24,16},{28,20},{1,9},{5... | collective-permute-start | bytes 1327112 | tf_op jit(solution)/shard_map/ppermute | solution.py:39
  246.9 21.0 %collective-permute-start.24 = (bf16[4,48,1152]{2,1,0:T(8,128)(2,1)}, bf16[4,48,1152]{2,1,0:T(8,128)(2,1)S(1)}, u32[]{:S(2)}, u32[]{:S(2)}) collective-permute-start(bf16[4,48,1152]{2,1,0:T(8,128)(2,1)} %get-tuple-element.179), channel_id=1, source_target_pairs={{0,16},{4,20},{8,24},{12,28},{16,0},{20,4},{24,8},{28,12},{1,17},{... | collective-permute-start | bytes 1327112 | tf_op jit(solution)/shard_map/ppermute | solution.py:39
  248.7 20.9 %collective-permute-start.25 = (bf16[4,48,1152]{2,1,0:T(8,128)(2,1)}, bf16[4,48,1152]{2,1,0:T(8,128)(2,1)}, u32[]{:S(2)}, u32[]{:S(2)}) collective-permute-start(bf16[4,48,1152]{2,1,0:T(8,128)(2,1)} %get-tuple-element.178), channel_id=1, source_target_pairs={{0,24},{4,28},{8,16},{12,20},{16,8},{20,12},{24,0},{28,4},{1,25},{... | collective-permute-start | bytes 1327112 | tf_op jit(solution)/shard_map/ppermute | solution.py:39
  250.4 20.4 %collective-permute-start.27 = (bf16[48,2304]{1,0:T(8,128)(2,1)}, bf16[48,2304]{1,0:T(8,128)(2,1)S(1)}, u32[]{:S(2)}, u32[]{:S(2)}) collective-permute-start(bf16[48,2304]{1,0:T(8,128)(2,1)} %get-tuple-element.184), channel_id=1, source_target_pairs={{0,1},{1,0},{2,3},{3,2},{4,5},{5,4},{6,7},{7,6},{8,9},{9,8},{10,11... | collective-permute-start | bytes 663560 | tf_op jit(solution)/shard_map/ppermute | solution.py:39
  250.4 20.4 %collective-permute-start.28 = (bf16[48,2304]{1,0:T(8,128)(2,1)}, bf16[48,2304]{1,0:T(8,128)(2,1)S(1)}, u32[]{:S(2)}, u32[]{:S(2)}) collective-permute-start(bf16[48,2304]{1,0:T(8,128)(2,1)} %get-tuple-element.186), channel_id=1, source_target_pairs={{0,2},{1,3},{2,0},{3,1},{4,6},{5,7},{6,4},{7,5},{8,10},{9,11},{10,... | collective-permute-start | bytes 663560 | tf_op jit(solution)/shard_map/ppermute | solution.py:39
  277.7 9.6 %collective-permute-start.30 = (bf16[48,1152]{1,0:T(8,128)(2,1)S(1)}, bf16[48,1152]{1,0:T(8,128)(2,1)S(1)}, u32[]{:S(2)}, u32[]{:S(2)}) collective-permute-start(bf16[48,1152]{1,0:T(8,128)(2,1)S(1)} %get-tuple-element.193), channel_id=1, source_target_pairs={{0,2},{1,3},{2,0},{3,1},{4,6},{5,7},{6,4},{7,5},{8,10},{9,11},{10,... | collective-permute-start | bytes 331784 | tf_op jit(solution)/shard_map/ppermute | solution.py:39
  277.7 9.6 %collective-permute-start.31 = (bf16[48,1152]{1,0:T(8,128)(2,1)S(1)}, bf16[48,1152]{1,0:T(8,128)(2,1)S(1)}, u32[]{:S(2)}, u32[]{:S(2)}) collective-permute-start(bf16[48,1152]{1,0:T(8,128)(2,1)S(1)} %get-tuple-element.192), channel_id=1, source_target_pairs={{0,3},{1,2},{2,1},{3,0},{4,7},{5,6},{6,5},{7,4},{8,11},{9,10},{10,... | collective-permute-start | bytes 331784 | tf_op jit(solution)/shard_map/ppermute | solution.py:39
  280.3 10.4 %collective-permute-start.35 = (bf16[48,2304]{1,0:T(8,128)(2,1)S(1)}, bf16[48,2304]{1,0:T(8,128)(2,1)S(1)}, u32[]{:S(2)}, u32[]{:S(2)}) collective-permute-start(bf16[48,2304]{1,0:T(8,128)(2,1)S(1)} %get-tuple-element.165), channel_id=1, source_target_pairs={{0,24},{4,28},{8,16},{12,20},{16,8},{20,12},{24,0},{28,4},{1,25},{... | collective-permute-start | bytes 663560 | tf_op jit(solution)/shard_map/ppermute | solution.py:39
  281.8 11.5 %collective-permute-start.34 = (bf16[48,2304]{1,0:T(8,128)(2,1)S(1)}, bf16[48,2304]{1,0:T(8,128)(2,1)S(1)}, u32[]{:S(2)}, u32[]{:S(2)}) collective-permute-start(bf16[48,2304]{1,0:T(8,128)(2,1)S(1)} %get-tuple-element.165), channel_id=1, source_target_pairs={{0,16},{4,20},{8,24},{12,28},{16,0},{20,4},{24,8},{28,12},{1,17},{... | collective-permute-start | bytes 663560 | tf_op jit(solution)/shard_map/ppermute | solution.py:39
  283.5 9.8 %collective-permute-start.33 = (bf16[48,2304]{1,0:T(8,128)(2,1)S(1)}, bf16[48,2304]{1,0:T(8,128)(2,1)S(1)}, u32[]{:S(2)}, u32[]{:S(2)}) collective-permute-start(bf16[48,2304]{1,0:T(8,128)(2,1)S(1)} %get-tuple-element.165), channel_id=1, source_target_pairs={{0,8},{4,12},{8,0},{12,4},{16,24},{20,28},{24,16},{28,20},{1,9},{5... | collective-permute-start | bytes 663560 | tf_op jit(solution)/shard_map/ppermute | solution.py:39
  295.8 10.5 %collective-permute-start.38 = (bf16[192,1152]{1,0:T(8,128)(2,1)S(1)}, bf16[192,1152]{1,0:T(8,128)(2,1)S(1)}, u32[]{:S(2)}, u32[]{:S(2)}) collective-permute-start(bf16[192,1152]{1,0:T(8,128)(2,1)S(1)} %bitcast.97), channel_id=1, source_target_pairs={{0,4},{4,0},{8,12},{12,8},{16,20},{20,16},{24,28},{28,24},{1,5},{5... | collective-permute-start | bytes 1327112 | tf_op jit(solution)/shard_map/ppermute | solution.py:39
  (39 other events, 219.2 us)

commit v2 on v1

--- a/solution.py
+++ b/solution.py
@@ -65,15 +65,10 @@
     return count == 8 and shards == 4
 
 
-def halves(weight, core):
+def own_block(weight, start, rows):
     width = weight.shape[1] // 2
-    return lax.dynamic_slice_in_dim(weight, core * width, width, 1)
-
-
-def quarter_rows(block):
-    quarters = lax.axis_size("seq") // 2
-    rows = block.shape[0] // quarters
-    return lax.dynamic_slice_in_dim(block, (lax.axis_index("seq") // 2) * rows, rows, 0)
+    core = lax.axis_index("seq") % 2
+    return lax.dynamic_slice(weight, (start, core * width), (rows, width)).astype(bf16)
 
 
 def stack(part, axis, unit, then=()):
@@ -82,15 +77,19 @@
     return [part] + others
 
 
+def doubled(part, flip):
+    return jnp.concatenate([part, swap(part, "shard", flip)], axis=0)
+
+
 def down_rows(quarter):
     return 72 * quarter + 8 * (quarter % 2)
 
 
-def down_part(block, rows):
-    quarter = lax.axis_index("seq") // 2
-    padded = jnp.pad(block, ((0, 16), (0, 0)))
-    part = lax.dynamic_slice_in_dim(padded, down_rows(quarter), 80, 0)
-    return pack_down(part[None], rows)
+def down_part(weight, rows):
+    start = down_rows(lax.axis_index("seq") // 2)
+    last = jnp.minimum(start + 64, weight.shape[0] - 16)
+    block = jnp.concatenate([own_block(weight, start, 64), own_block(weight, last, 16)], axis=0)
+    return pack_down(block[None], rows)
 
 
 def pack_down(blocks, rows):
@@ -140,6 +139,12 @@
 
 def shard_pieces(half):
     return pieces(half, "shard", 1, lax.axis_index("shard"), lax.axis_size("shard"), 0)
+
+
+def halve(value, bit):
+    side = lax.axis_index("shard") & bit
+    kept_half = lax.dynamic_slice_in_dim(value, side, bit, 0)
+    return kept_half, swap(lax.dynamic_slice_in_dim(value, side ^ bit, bit, 0), "shard", bit)
 
 
 def owners_half(part, then=()):
@@ -909,14 +914,6 @@
     rows, width = tokens.shape
     device = lax.axis_index(("seq", "shard"))
     last_device = lax.axis_size(("seq", "shard")) - 1
-    cos, sin = rope_tables(positions, width // HEADS)
-    start = jnp.max(jnp.where(positions == 0, jnp.arange(rows, dtype=jnp.int32), 0))
-    low = jnp.where(device > 0, -HALF, 0)
-    high = jnp.where(device < last_device, rows + HALF, rows)
-    meta = jnp.stack([start, low, high]).astype(jnp.int32)
-    edge_x, edge_cos, edge_sin = (
-        jnp.concatenate(edge_rows(value), axis=0) for value in (tokens, cos, sin)
-    )
     shards = lax.axis_size("shard")
     quarters = lax.axis_size("seq") // 2
     core = lax.axis_index("seq") % 2
@@ -928,36 +925,46 @@
     rest = down_weight.shape[0] // quarters - slot
     wide = mlp_weight.shape[1] // 2
     down_at = wide + attn_weight.shape[1] // 2
-    lows = [w.astype(bf16) for w in (qkv_weight, attn_weight, mlp_weight, down_weight)]
+    quarter = lax.axis_index("seq") // 2
+    edge_x = jnp.concatenate(edge_rows(tokens), axis=0)
     if split:
-        qkv_low, attn_low, mlp_low, down_low = lows
-        part = quarter_rows(halves(qkv_low, core))
+        part = own_block(qkv_weight, quarter * slot, slot)
         gain_rows = jnp.pad(norm_gains.astype(bf16), ((0, 6), (0, half - norm_gains.shape[1])))
         qkv_stack = stack(jnp.concatenate([part, gain_rows], axis=0), "shard", 1)
+        rest_part = jnp.concatenate(
+            [own_block(w, quarter * slot, slot) for w in (mlp_weight, attn_weight)]
+            + down_part(down_weight, slot),
+            axis=1,
+        )
+        qkv_part = jnp.concatenate([piece[:slot] for piece in qkv_stack], axis=0)
+        rest_part = doubled(rest_part, 1)
+        qkv_part = after(qkv_part, rest_part)
+        rest_part = doubled(rest_part, 2)
+        qkv_pieces = stack(qkv_part, "seq", 2)
+        positions, edge_x = after((positions, edge_x), qkv_part)
         gains = jnp.zeros((shards, 2, norm_gains.shape[1]), bf16)
         for d, piece in enumerate(qkv_stack):
             piece = piece[None, slot : slot + 2, : norm_gains.shape[1]]
             gains = lax.dynamic_update_slice_in_dim(gains, piece, lax.axis_index("shard") ^ d, 0)
         gains = gains.astype(f32).transpose(1, 0, 2).reshape(2, -1)
-        rest_part = jnp.concatenate(
-            [quarter_rows(halves(w, core)) for w in (mlp_low, attn_low)]
-            + down_part(halves(down_low, core), slot),
-            axis=1,
-        )
-        rest_part = jnp.concatenate(
-            stack(after(rest_part, qkv_stack[1]), "shard", 1), axis=0
-        )
-        qkv_part = jnp.concatenate([piece[:slot] for piece in qkv_stack], axis=0)
-        qkv_part = jnp.concatenate(stack(qkv_part, "seq", 2), axis=0)
-        qkv_part = after(qkv_part, rest_part, gains, meta, place, edge_x, edge_cos, edge_sin)
-        rest_part = after(rest_part, qkv_part)
-        qkv_parts = qkv_part, swap(qkv_part, "seq", 1)
     else:
+        lows = [w.astype(bf16) for w in (qkv_weight, attn_weight, mlp_weight, down_weight)]
         full_qkv, full_attn, full_mlp, full_down = (
             lax.all_gather(w, "shard", axis=0, tiled=True) for w in lows
         )
         gains = lax.all_gather(norm_gains.astype(bf16), "shard", axis=1, tiled=True).astype(f32)
         qkv_parts = (full_qkv,)
+    cos, sin = rope_tables(positions, width // HEADS)
+    start = jnp.max(jnp.where(positions == 0, jnp.arange(rows, dtype=jnp.int32), 0))
+    low = jnp.where(device > 0, -HALF, 0)
+    high = jnp.where(device < last_device, rows + HALF, rows)
+    meta = jnp.stack([start, low, high]).astype(jnp.int32)
+    edge_cos, edge_sin = (jnp.concatenate(edge_rows(value), axis=0) for value in (cos, sin))
+    if split:
+        qkv_pieces = after(qkv_pieces, rest_part, gains, meta, place, edge_x, edge_cos, edge_sin)
+        qkv_part = jnp.concatenate(qkv_pieces, axis=0)
+        rest_part = after(rest_part, qkv_part)
+        qkv_parts = qkv_part, swap(qkv_part, "seq", 1)
     kv_head, kv_tail, full_qkv = project_edges(
         split, place, edge_x, gains, edge_cos, edge_sin, *qkv_parts
     )
@@ -1008,11 +1015,13 @@
         qkv_half = keep_half(qkv_own, qkv_got)
         dq = after(dq, qkv_half)
         qkv_pieces = quarter_pieces(qkv_half)
-        rest_pieces = shard_pieces(rest_part)
+        rest_pieces = halve(rest_part, 2)
     input_grad = input_gradient(tokens, gains, full_qkv, dmid, dq, dk, dv, edge_k, edge_v)
     if split:
         qkv_part = sum_after(qkv_pieces, input_grad)
-        rest_part = sum_after(rest_pieces, qkv_part)
+        rest_part = sum_after(list(rest_pieces), qkv_part)
+        rest_pieces = halve(rest_part, 1)
+        rest_part = sum_after(list(rest_pieces), qkv_part)[0]
         qkv_part = sum_after(shard_pieces(qkv_part), rest_part)
         rest_half = owners_half(rest_part, (qkv_part,))
         rest_got = swap(rest_half, "seq", 1)

time: 312 us -> 300 us (0.962)
  waiting for transfers between devices: 39.8 us -> 55.5 us
  starting transfers between devices: 56.1 us -> 45.8 us
  local copies, waits for them, and re-layouts: 33.9 us -> 23.7 us
  other arithmetic: 36.9 us -> 29.8 us
    ppermute x36 -> x34, waiting for transfers between devices: 39.8 us -> 55.5 us  [swap(): return lax.ppermute(value, axis, [(i, i ^ flip) for i in range(count)])]
    ppermute x36 -> x34, starting transfers between devices: 43.4 us -> 32.6 us  [swap(): return lax.ppermute(value, axis, [(i, i ^ flip) for i in range(count)])]
    dynamic_slice x2 -> x7, local copies, waits for them, and re-layouts: 1.72 us -> 5.37 us  [the longest x5 4.55 us: own_block(): lax.dynamic_slice(weight, (start, core * width), (rows, width)).astype(bf16)]
    unnamed x68 -> x60, local copies, waits for them, and re-layouts: 15.6 us -> 12 us
    convert_element_type x4 -> x5, other arithmetic: 8.75 us -> 8.96 us  [total_of(): return total.astype(bf16)]
  transfers between devices with their start and end apart: 40 -> 38, of which waited for: 16 -> 20; matrix products, arithmetic and copies ran while one was open for 13% -> 8% of each run, Pallas kernels for 27% -> 28%
where the time goes in v2:
time: 300 us
  Pallas kernels  144 us (48%)
  waiting for transfers between devices  55.5 us (18%)
  starting transfers between devices  45.8 us (15%)
  other arithmetic  29.8 us (10%)
  local copies, waits for them, and re-layouts  23.7 us (8%)
    pallas_call x1, Pallas kernels, middle(): call(functools.partial(middle_kernel, split), rows // tile, [pl.BlockSpec...  59.4 us
    ppermute x34, waiting for transfers between devices, swap(): return lax.ppermute(value, axis, [(i, i ^ flip) for i in range(count)])  55.5 us
    ppermute x34, starting transfers between devices, swap(): return lax.ppermute(value, axis, [(i, i ^ flip) for i in range(count)])  32.6 us
    pallas_call x1, Pallas kernels, attend_back(): call(attend_back_kernel, steps, back_specs(rows, steps) + [pairs(2 * ROWS...  19.5 us
    pallas_call x2, Pallas kernels, attend(): call(attend_kernel, count, [pl.BlockSpec(memory_space=pltpu.SMEM)] + [col...  18 us
    unnamed x60, local copies, waits for them, and re-layouts  12 us
    pallas_call x1, Pallas kernels, input_gradient(): call(input_kernel, rows // tile, [tiles(tile, width), held(2, width), kep...  11.3 us
    pallas_call x1, Pallas kernels, qkv_gradient(): call(functools.partial(qkv_grad_kernel, split), rows // tile, [pl.BlockSp...  11.1 us
  transfers between devices with their start and end apart: 38, of which 20 were waited for; matrix products, arithmetic and copies ran while one was open for 8% of the time, Pallas kernels for 28%

profile of v2, /device:TPU:0, one launch (start us, length us, event | category | flops | bytes accessed | tf_op | source)
XLA Modules:
  0.0 300.5 jit_solution(9725955126808450249)
XLA Ops:
  2.3 3.1 %collective-permute-start = (bf16[56,1152]{1,0:T(8,128)(2,1)S(1)}, bf16[56,1152]{1,0:T(8,128)(2,1)S(1)}, u32[]{:S(2)}, u32[]{:S(2)}) collective-permute-start(bf16[56,1152]{1,0:T(8,128)(2,1)S(1)} %fusion.21), channel_id=1, source_target_pairs={{0,1},{1,0},{2,3},{3,2},{4,5},{5,4},{6,7},{7,6},{8,9},{9,8},{10,11... | collective-permute-start | bytes 387080 | tf_op jit(solution)/shard_map/ppermute | solution.py:39
  5.4 2.6 collective-permute-start.1
  15.9 2.4 collective-permute-done.1
  19.2 2.3 collective-permute-done.3
  26.4 2.4 fusion.14
  31.4 3.9 %collective-permute-done.4 = bf16[192,1152]{1,0:T(8,128)(2,1)S(1)} collective-permute-done((bf16[192,1152]{1,0:T(8,128)(2,1)S(1)}, bf16[192,1152]{1,0:T(8,128)(2,1)S(1)}, u32[]{:S(2)}, u32[]{:S(2)}) %collective-permute-start.4) | collective-permute-done | bytes 442400 | tf_op jit(solution)/shard_map/ppermute | solution.py:39
  35.3 8.9 %collective-permute-done.5 = bf16[192,1152]{1,0:T(8,128)(2,1)S(1)} collective-permute-done((bf16[192,1152]{1,0:T(8,128)(2,1)S(1)}, bf16[192,1152]{1,0:T(8,128)(2,1)S(1)}, u32[]{:S(2)}, u32[]{:S(2)}) %collective-permute-start.5) | collective-permute-done | bytes 442400 | tf_op jit(solution)/shard_map/ppermute | solution.py:39
  50.4 5.1 %shard_map.305 = (bf16[64,1536]{1,0:T(8,128)(2,1)}, bf16[64,1536]{1,0:T(8,128)(2,1)}, bf16[768,2304]{1,0:T(8,128)(2,1)}) custom-call(s32[3]{0:T(128)} %pad_add_fusion.place_ref, bf16[128,768]{1,0:T(8,128)(2,1)} %pad_maximum_fusion.10.x_ref, f32[2,768]{1,0:T(2,128)} %reshape.109.gain_ref, f32[128,128]{1,0:T(8,128)} %pad_maximum_fusion.11.cos_ref, ...), custom_call_target="tpu_custom_call" | custom-call | flops 4718592 | bytes 119808 | tf_op jit(solution)/shard_map/pallas_call | solution.py:701
  56.8 5.4 %collective-permute-start.10 = (bf16[64,1536]{1,0:T(8,128)(2,1)}, bf16[64,1536]{1,0:T(8,128)(2,1)S(1)}, u32[]{:S(2)}, u32[]{:S(2)}) collective-permute-start(bf16[64,1536]{1,0:T(8,128)(2,1)} %get-tuple-element.101), channel_id=1, source_target_pairs={{0,1},{1,2},{2,3},{3,4},{4,5},{5,6},{6,7},{7,8},{8,9},{9,10},{10,1... | collective-permute-start | bytes 589832 | tf_op jit(solution)/shard_map/ppermute | solution.py:169
  63.4 10.1 %shard_map.306 = (bf16[1280,768]{1,0:T(8,128)(2,1)}, bf16[1280,768]{1,0:T(8,128)(2,1)}, bf16[1280,768]{1,0:T(8,128)(2,1)}, bf16[1280,768]{1,0:T(8,128)(2,1)}) custom-call(bf16[1280,768]{1,0:T(8,128)(2,1)} %x_ref.4, f32[2,768]{1,0:T(2,128)} %reshape.109.gain_ref, bf16[768,2304]{1,0:T(8,128)(2,1)} %get-tuple-element.96.w_ref, f32[1280,128]{1,0:T(8,128)} %copy-done.3, ...), custom_call_target="tpu_custom_call" | custom-call | flops 70778880 | bytes 208896 | tf_op jit(solution)/shard_map/pallas_call | solution.py:687
  74.3 8.5 %shard_map.307 = (bf16[768,1280]{1,0:T(8,128)(2,1)}, f32[6,10,256]{2,1,0:T(8,128)}) custom-call(s32[3]{0:T(128)} %pad_add_fusion.1.meta_ref, bf16[1280,768]{1,0:T(8,128)(2,1)} %get-tuple-element.108.q_ref, bf16[1280,768]{1,0:T(8,128)(2,1)} %get-tuple-element.99.k_ref, bf16[1280,768]{1,0:T(8,128)(2,1)} %get-tuple-element.100.v_ref, ...), custom_call_target="tpu_custom_call" | custom-call | flops 31457280 | bytes 122880 | tf_op jit(solution)/shard_map/pallas_call | solution.py:732
  82.9 5.3 %collective-permute-done.12 = bf16[192,2304]{1,0:T(8,128)(2,1)} collective-permute-done((bf16[192,2304]{1,0:T(8,128)(2,1)}, bf16[192,2304]{1,0:T(8,128)(2,1)}, u32[]{:S(2)}, u32[]{:S(2)}) %collective-permute-start.12) | collective-permute-done | bytes 884768 | tf_op jit(solution)/shard_map/ppermute | solution.py:39
  93.8 9.5 %shard_map.308 = (bf16[768,1280]{1,0:T(8,128)(2,1)}, f32[6,10,256]{2,1,0:T(8,128)}) custom-call(s32[3]{0:T(128)} %pad_add_fusion.1.meta_ref, bf16[1280,768]{1,0:T(8,128)(2,1)} %get-tuple-element.108.q_ref, bf16[1280,768]{1,0:T(8,128)(2,1)} %get-tuple-element.99.k_ref, ...), custom_call_target="tpu_custom_call", output_to_operand_aliasing={{0}: (8, {}), {1}: (9, {})} | custom-call | flops 31457280 | bytes 122880 | tf_op jit(solution)/shard_map/pallas_call | solution.py:732
  103.2 59.4 %shard_map.309 = (bf16[1280,768]{1,0:T(8,128)(2,1)}, bf16[1280,768]{1,0:T(8,128)(2,1)}, bf16[1280,768]{1,0:T(8,128)(2,1)}, bf16[768,2304]{1,0:T(8,128)(2,1)}, bf16[768,2304]{1,0:T(8,128)(2,1)}) custom-call(s32[3]{0:T(128)} %pad_add_fusion.place_ref, bf16[1280,768]{1,0:T(8,128)(2,1)} %x_ref.4, bf16[768,1280]{1,0:T(8,128)(2,1)} %get-tuple-element.110.o_ref, ...), custom_call_target="tpu_custom_call" | custom-call | flops 353894400 | bytes 399360 | tf_op jit(solution)/shard_map/pallas_call | solution.py:811
  162.7 9.5 %shard_map.310 = (bf16[256,768]{1,0:T(8,128)(2,1)}, f32[512,768]{1,0:T(8,128)}, f32[512,768]{1,0:T(8,128)}, bf16[2,64,768]{2,1,0:T(8,128)(2,1)}, bf16[2,64,768]{...) custom-call(s32[3]{0:T(128)} %pad_add_fusion.1.meta_ref, bf16[1280,768]{1,0:T(8,128)(2,1)} %get-tuple-element.108.q_ref, ...), custom_call_target="tpu_custom_call" | custom-call | flops 15728640 | bytes 153600 | tf_op jit(solution)/shard_map/pallas_call | solution.py:769
  174.0 3.9 %add_convert_fusion = bf16[768,2304]{1,0:T(8,128)(2,1)S(1)} fusion(bf16[768,2304]{1,0:T(8,128)(2,1)} %copy-done.6, bf16[768,2304]{1,0:T(8,128)(2,1)} %get-tuple-element.114), kind=kLoop, calls=%fused_computation | loop fusion | flops 7077888 | bytes 10616832 | tf_op jit(solution)/shard_map/convert_element_type | solution.py:117
  180.5 2.5 collective-permute-start.20
  184.3 5.3 %collective-permute-start.16 = (bf16[2,64,768]{2,1,0:T(8,128)(2,1)}, bf16[2,64,768]{2,1,0:T(8,128)(2,1)}, u32[]{:S(2)}, u32[]{:S(2)}) collective-permute-start(bf16[2,64,768]{2,1,0:T(8,128)(2,1)} %get-tuple-element.129), channel_id=1, source_target_pairs={{0,1},{1,2},{2,3},{3,4},{4,5},{5,6},{6,7},{7,8},{8,9},{9,10},{10,1... | collective-permute-start | bytes 589832 | tf_op jit(solution)/shard_map/ppermute | solution.py:169
  189.6 19.5 %shard_map.311 = (bf16[1280,768]{1,0:T(8,128)(2,1)}, bf16[1280,768]{1,0:T(8,128)(2,1)}, bf16[1280,768]{1,0:T(8,128)(2,1)}) custom-call(s32[3]{0:T(128)} %pad_add_fusion.1.meta_ref, bf16[1280,768]{1,0:T(8,128)(2,1)} %get-tuple-element.108.q_ref, bf16[1280,768]{1,0:T(8,128)(2,1)} %get-tuple-element.99.k_ref, bf16[1280,768]{1,0:T(8,128)(2,1)} %get-tuple-element.100.v_ref, ...), custom_call_target="tpu_custom_call" | custom-call | flops 78643200 | bytes 215040 | tf_op jit(solution)/shard_map/pallas_call | solution.py:791
  209.1 11.1 %shard_map.312 = (bf16[128,768]{1,0:T(8,128)(2,1)}, bf16[128,768]{1,0:T(8,128)(2,1)}, bf16[768,1152]{1,0:T(8,128)(2,1)}, bf16[768,1152]{1,0:T(8,128)(2,1)}) custom-call(s32[3]{0:T(128)} %pad_add_fusion.place_ref, bf16[1280,768]{1,0:T(8,128)(2,1)} %get-tuple-element.124.h_ref, bf16[1280,768]{1,0:T(8,128)(2,1)} %get-tuple-element.138.dq_ref, ...), custom_call_target="tpu_custom_call" | custom-call | flops 70778880 | bytes 178176 | tf_op jit(solution)/shard_map/pallas_call | solution.py:835
  221.1 3.2 %fusion.8 = bf16[4,48,2304]{2,1,0:T(8,128)(2,1)} fusion(bf16[4,48,2304]{2,1,0:T(8,128)(2,1)} %collective-permute-done.20, bf16[4,48,2304]{2,1,0:T(8,128)(2,1)} %collective-permute-done.19, bf16[4,48,2304]{2,1,0:T(8,128)(2,1)} %collective-permute-done.18, bf16[4,4,48,2304]{3,2,1,0:T(8,128)(2,1)S(1)} %bitcast.81, s32[]{:T(128)S(6)} %select_n.176), kind=kLoop, calls=%fused_computation.19 | loop fusion | flops 3538944 | bytes 4423684 | tf_op jit(solution)/shard_map/convert_element_type | solution.py:117
  224.3 3.7 %collective-permute-done.21 = bf16[768,1152]{1,0:T(8,128)(2,1)S(1)} collective-permute-done((bf16[768,1152]{1,0:T(8,128)(2,1)S(1)}, bf16[768,1152]{1,0:T(8,128)(2,1)S(1)}, u32[]{:S(2)}, u32[]{:S(2)}) %collective-permute-start.21) | collective-permute-done | bytes 1769504 | tf_op jit(solution)/shard_map/ppermute | solution.py:39
  229.6 2.1 collective-permute-start.22
  235.0 11.3 %shard_map.313 = bf16[1280,768]{1,0:T(8,128)(2,1)} custom-call(bf16[1280,768]{1,0:T(8,128)(2,1)} %x_ref.4, f32[2,768]{1,0:T(2,128)} %reshape.109.gain_ref, bf16[768,2304]{1,0:T(8,128)(2,1)} %get-tuple-element.96.w_ref, bf16[1280,768]{1,0:T(8,128)(2,1)} %get-tuple-element.112.dmid_ref, bf16[1280,768]{1,0:T(8,128)(2,1)} %get-tuple-element.138.dq_ref, ...), custom_call_target="tpu_custom_call" | custom-call | flops 70778880 | bytes 270336 | tf_op jit(solution)/shard_map/pallas_call | solution.py:854
  246.3 6.2 %collective-permute-done.23 = bf16[4,48,1152]{2,1,0:T(8,128)(2,1)S(1)} collective-permute-done((bf16[4,48,1152]{2,1,0:T(8,128)(2,1)}, bf16[4,48,1152]{2,1,0:T(8,128)(2,1)S(1)}, u32[]{:S(2)}, u32[]{:S(2)}) %collective-permute-start.23) | collective-permute-done | bytes 442400 | tf_op jit(solution)/shard_map/ppermute | solution.py:39
  257.4 2.1 collective-permute-start.25
  259.4 2.4 collective-permute-start.29
  261.9 6.1 %collective-permute-done.27 = bf16[1,48,2304]{2,1,0:T(8,128)(2,1)S(1)} collective-permute-done((bf16[1,48,2304]{2,1,0:T(8,128)(2,1)S(1)}, bf16[1,48,2304]{2,1,0:T(8,128)(2,1)S(1)}, u32[]{:S(2)}, u32[]{:S(2)}) %collective-permute-start.27) | collective-permute-done | bytes 221216 | tf_op jit(solution)/shard_map/ppermute | solution.py:39
  269.6 2.1 collective-permute-done.25
  277.4 3.8 %collective-permute-done.32 = bf16[48,2304]{1,0:T(8,128)(2,1)S(1)} collective-permute-done((bf16[48,2304]{1,0:T(8,128)(2,1)S(1)}, bf16[48,2304]{1,0:T(8,128)(2,1)S(1)}, u32[]{:S(2)}, u32[]{:S(2)}) %collective-permute-start.32) | collective-permute-done | bytes 221216 | tf_op jit(solution)/shard_map/ppermute | solution.py:39
  286.9 3.4 %multiply_subtract_fusion = (f32[192,2304]{1,0:T(8,128)}, f32[192,2304]{1,0:T(8,128)}, f32[192,2304]{1,0:T(8,128)}, f32[192]{0:T(256)S(1)}) fusion(f32[192,2304]{1,0:T(8,128)S(1)} %copy-done.8, bf16[192,1152]{1,0:T(8,128)(2,1)S(1)} %slice.122, bf16[192,1152]{1,0:T(8,128)(2,1)S(1)} %slice.121, f32[192,2304]{1,0:T(8,128)S(1)} %copy-done.12, ...), kind=kLoop, calls=%fused_computation.20 | loop fusion | flops 10174272 | bytes 11502336 | tf_op jit(solution)/shard_map/sub | solution.py:884
  296.3 3.4 %multiply_subtract_fusion.1 = (f32[192,2304]{1,0:T(8,128)}, f32[192,2304]{1,0:T(8,128)}, f32[192,2304]{1,0:T(8,128)}, f32[192]{0:T(256)S(1)}) fusion(f32[192,2304]{1,0:T(8,128)S(1)} %copy-done.9, bf16[192,1152]{1,0:T(8,128)(2,1)S(1)} %get-tuple-element.187, bf16[192,1152]{1,0:T(8,128)(2,1)S(1)} %get-tuple-element.186, f32[192,2304]{1,0:T(8,128)S(1)} %copy-done.14, ...), kind=kLoop, calls=%fused_computation.21 | loop fusion | flops 10174272 | bytes 11502336 | tf_op jit(solution)/shard_map/sub | solution.py:884
  (202 shorter events, 68.4 us)
Async XLA Ops:
  2.3 13.5 %collective-permute-start = (bf16[56,1152]{1,0:T(8,128)(2,1)S(1)}, bf16[56,1152]{1,0:T(8,128)(2,1)S(1)}, u32[]{:S(2)}, u32[]{:S(2)}) collective-permute-start(bf16[56,1152]{1,0:T(8,128)(2,1)S(1)} %fusion.21), channel_id=1, source_target_pairs={{0,1},{1,0},{2,3},{3,2},{4,5},{5,4},{6,7},{7,6},{8,9},{9,8},{10,11... | collective-permute-start | bytes 387080 | tf_op jit(solution)/shard_map/ppermute | solution.py:39
  5.4 12.8 %collective-permute-start.1 = (bf16[56,1152]{1,0:T(8,128)(2,1)S(1)}, bf16[56,1152]{1,0:T(8,128)(2,1)S(1)}, u32[]{:S(2)}, u32[]{:S(2)}) collective-permute-start(bf16[56,1152]{1,0:T(8,128)(2,1)S(1)} %fusion.21), channel_id=1, source_target_pairs={{0,2},{1,3},{2,0},{3,1},{4,6},{5,7},{6,4},{7,5},{8,10},{9,11},{10,... | collective-permute-start | bytes 387080 | tf_op jit(solution)/shard_map/ppermute | solution.py:39
  8.0 10.2 %collective-permute-start.2 = (bf16[56,1152]{1,0:T(8,128)(2,1)S(1)}, bf16[56,1152]{1,0:T(8,128)(2,1)S(1)}, u32[]{:S(2)}, u32[]{:S(2)}) collective-permute-start(bf16[56,1152]{1,0:T(8,128)(2,1)S(1)} %fusion.21), channel_id=1, source_target_pairs={{0,3},{1,2},{2,1},{3,0},{4,7},{5,6},{6,5},{7,4},{8,11},{9,10},{10,... | collective-permute-start | bytes 387080 | tf_op jit(solution)/shard_map/ppermute | solution.py:39
  11.7 9.8 %collective-permute-start.3 = (bf16[48,2304]{1,0:T(8,128)(2,1)S(1)}, bf16[48,2304]{1,0:T(8,128)(2,1)S(1)}, u32[]{:S(2)}, u32[]{:S(2)}) collective-permute-start(bf16[48,2304]{1,0:T(8,128)(2,1)S(1)} %pad_maximum_fusion.7), channel_id=1, source_target_pairs={{0,1},{1,0},{2,3},{3,2},{4,5},{5,4},{6,7},{7,6},{8,9},{9,8},{10,11... | collective-permute-start | bytes 663560 | tf_op jit(solution)/shard_map/ppermute | solution.py:39
  21.5 22.7 %collective-permute-start.7 = (bf16[96,2304]{1,0:T(8,128)(2,1)S(1)}, bf16[96,2304]{1,0:T(8,128)(2,1)S(1)}, u32[]{:S(2)}, u32[]{:S(2)}) collective-permute-start(bf16[96,2304]{1,0:T(8,128)(2,1)S(1)} %pad_maximum_fusion.4), channel_id=1, source_target_pairs={{0,2},{1,3},{2,0},{3,1},{4,6},{5,7},{6,4},{7,5},{8,10},{9,11},{10,... | collective-permute-start | bytes 1327112 | tf_op jit(solution)/shard_map/ppermute | solution.py:39
  22.2 13.1 %collective-permute-start.4 = (bf16[192,1152]{1,0:T(8,128)(2,1)S(1)}, bf16[192,1152]{1,0:T(8,128)(2,1)S(1)}, u32[]{:S(2)}, u32[]{:S(2)}) collective-permute-start(bf16[192,1152]{1,0:T(8,128)(2,1)S(1)} %pad_maximum_fusion.3), channel_id=1, source_target_pairs={{0,8},{4,12},{8,0},{12,4},{16,24},{20,28},{24,16},{28,20},{1,9},{5... | collective-permute-start | bytes 1327112 | tf_op jit(solution)/shard_map/ppermute | solution.py:39
  23.7 20.5 %collective-permute-start.5 = (bf16[192,1152]{1,0:T(8,128)(2,1)S(1)}, bf16[192,1152]{1,0:T(8,128)(2,1)S(1)}, u32[]{:S(2)}, u32[]{:S(2)}) collective-permute-start(bf16[192,1152]{1,0:T(8,128)(2,1)S(1)} %pad_maximum_fusion.3), channel_id=1, source_target_pairs={{0,16},{4,20},{8,24},{12,28},{16,0},{20,4},{24,8},{28,12},{1,17},{... | collective-permute-start | bytes 1327112 | tf_op jit(solution)/shard_map/ppermute | solution.py:39
  25.2 20.0 %collective-permute-start.6 = (bf16[192,1152]{1,0:T(8,128)(2,1)S(1)}, bf16[192,1152]{1,0:T(8,128)(2,1)S(1)}, u32[]{:S(2)}, u32[]{:S(2)}) collective-permute-start(bf16[192,1152]{1,0:T(8,128)(2,1)S(1)} %pad_maximum_fusion.3), channel_id=1, source_target_pairs={{0,24},{4,28},{8,16},{12,20},{16,8},{20,12},{24,0},{28,4},{1,25},{... | collective-permute-start | bytes 1327112 | tf_op jit(solution)/shard_map/ppermute | solution.py:39
  45.5 37.3 %collective-permute-start.13 = (bf16[192,2304]{1,0:T(8,128)(2,1)}, bf16[192,2304]{1,0:T(8,128)(2,1)}, u32[]{:S(2)}, u32[]{:S(2)}) collective-permute-start(bf16[192,2304]{1,0:T(8,128)(2,1)} %pad_maximum_fusion), channel_id=1, source_target_pairs={{0,24},{4,28},{8,16},{12,20},{16,8},{20,12},{24,0},{28,4},{1,25},{... | collective-permute-start | bytes 2654216 | tf_op jit(solution)/shard_map/ppermute | solution.py:39
  47.1 41.1 %collective-permute-start.12 = (bf16[192,2304]{1,0:T(8,128)(2,1)}, bf16[192,2304]{1,0:T(8,128)(2,1)}, u32[]{:S(2)}, u32[]{:S(2)}) collective-permute-start(bf16[192,2304]{1,0:T(8,128)(2,1)} %pad_maximum_fusion), channel_id=1, source_target_pairs={{0,16},{4,20},{8,24},{12,28},{16,0},{20,4},{24,8},{28,12},{1,17},{... | collective-permute-start | bytes 2654216 | tf_op jit(solution)/shard_map/ppermute | solution.py:39
  47.6 42.4 %collective-permute-start.9 = (bf16[192,2304]{1,0:T(8,128)(2,1)}, bf16[192,2304]{1,0:T(8,128)(2,1)}, u32[]{:S(2)}, u32[]{:S(2)}) collective-permute-start(bf16[192,2304]{1,0:T(8,128)(2,1)} %pad_maximum_fusion), channel_id=1, source_target_pairs={{0,8},{4,12},{8,0},{12,4},{16,24},{20,28},{24,16},{28,20},{1,9},{5... | collective-permute-start | bytes 2654216 | tf_op jit(solution)/shard_map/ppermute | solution.py:39
  55.5 18.1 %collective-permute-start.11 = (bf16[64,1536]{1,0:T(8,128)(2,1)}, bf16[64,1536]{1,0:T(8,128)(2,1)S(1)}, u32[]{:S(2)}, u32[]{:S(2)}) collective-permute-start(bf16[64,1536]{1,0:T(8,128)(2,1)} %get-tuple-element.94), channel_id=1, source_target_pairs={{1,0},{2,1},{3,2},{4,3},{5,4},{6,5},{7,6},{8,7},{9,8},{10,9},{11,1... | collective-permute-start | bytes 589832 | tf_op jit(solution)/shard_map/ppermute | solution.py:175
  56.8 16.8 %collective-permute-start.10 = (bf16[64,1536]{1,0:T(8,128)(2,1)}, bf16[64,1536]{1,0:T(8,128)(2,1)S(1)}, u32[]{:S(2)}, u32[]{:S(2)}) collective-permute-start(bf16[64,1536]{1,0:T(8,128)(2,1)} %get-tuple-element.101), channel_id=1, source_target_pairs={{0,1},{1,2},{2,3},{3,4},{4,5},{5,6},{6,7},{7,8},{8,9},{9,10},{10,1... | collective-permute-start | bytes 589832 | tf_op jit(solution)/shard_map/ppermute | solution.py:169
  162.7 9.6 %collective-permute-start.15 = (bf16[768,2304]{1,0:T(8,128)(2,1)}, bf16[768,2304]{1,0:T(8,128)(2,1)S(1)}, u32[]{:S(2)}, u32[]{:S(2)}) collective-permute-start(bf16[768,2304]{1,0:T(8,128)(2,1)} %get-tuple-element.115), channel_id=1, source_target_pairs={{0,4},{4,0},{8,12},{12,8},{16,20},{20,16},{24,28},{28,24},{1,5},{5... | collective-permute-start | bytes 10616840 | tf_op jit(solution)/shard_map/ppermute | solution.py:39
  179.5 40.7 %collective-permute-start.18 = (bf16[4,48,2304]{2,1,0:T(8,128)(2,1)}, bf16[4,48,2304]{2,1,0:T(8,128)(2,1)}, u32[]{:S(2)}, u32[]{:S(2)}) collective-permute-start(bf16[4,48,2304]{2,1,0:T(8,128)(2,1)} %get-tuple-element.174), channel_id=1, source_target_pairs={{0,8},{4,12},{8,0},{12,4},{16,24},{20,28},{24,16},{28,20},{1,9},{5... | collective-permute-start | bytes 2654216 | tf_op jit(solution)/shard_map/ppermute | solution.py:39
  180.1 41.0 %collective-permute-start.19 = (bf16[4,48,2304]{2,1,0:T(8,128)(2,1)}, bf16[4,48,2304]{2,1,0:T(8,128)(2,1)}, u32[]{:S(2)}, u32[]{:S(2)}) collective-permute-start(bf16[4,48,2304]{2,1,0:T(8,128)(2,1)} %get-tuple-element.176), channel_id=1, source_target_pairs={{0,16},{4,20},{8,24},{12,28},{16,0},{20,4},{24,8},{28,12},{1,17},{... | collective-permute-start | bytes 2654216 | tf_op jit(solution)/shard_map/ppermute | solution.py:39
  180.5 40.5 %collective-permute-start.20 = (bf16[4,48,2304]{2,1,0:T(8,128)(2,1)}, bf16[4,48,2304]{2,1,0:T(8,128)(2,1)}, u32[]{:S(2)}, u32[]{:S(2)}) collective-permute-start(bf16[4,48,2304]{2,1,0:T(8,128)(2,1)} %get-tuple-element.175), channel_id=1, source_target_pairs={{0,24},{4,28},{8,16},{12,20},{16,8},{20,12},{24,0},{28,4},{1,25},{... | collective-permute-start | bytes 2654216 | tf_op jit(solution)/shard_map/ppermute | solution.py:39
  183.0 26.0 %collective-permute-start.17 = (bf16[2,64,768]{2,1,0:T(8,128)(2,1)}, bf16[2,64,768]{2,1,0:T(8,128)(2,1)}, u32[]{:S(2)}, u32[]{:S(2)}) collective-permute-start(bf16[2,64,768]{2,1,0:T(8,128)(2,1)} %get-tuple-element.117), channel_id=1, source_target_pairs={{1,0},{2,1},{3,2},{4,3},{5,4},{6,5},{7,6},{8,7},{9,8},{10,9},{11,1... | collective-permute-start | bytes 589832 | tf_op jit(solution)/shard_map/ppermute | solution.py:175
  184.3 24.8 %collective-permute-start.16 = (bf16[2,64,768]{2,1,0:T(8,128)(2,1)}, bf16[2,64,768]{2,1,0:T(8,128)(2,1)}, u32[]{:S(2)}, u32[]{:S(2)}) collective-permute-start(bf16[2,64,768]{2,1,0:T(8,128)(2,1)} %get-tuple-element.129), channel_id=1, source_target_pairs={{0,1},{1,2},{2,3},{3,4},{4,5},{5,6},{6,7},{7,8},{8,9},{9,10},{10,1... | collective-permute-start | bytes 589832 | tf_op jit(solution)/shard_map/ppermute | solution.py:169
  229.6 16.7 %collective-permute-start.22 = (bf16[4,48,1152]{2,1,0:T(8,128)(2,1)}, bf16[4,48,1152]{2,1,0:T(8,128)(2,1)S(1)}, u32[]{:S(2)}, u32[]{:S(2)}) collective-permute-start(bf16[4,48,1152]{2,1,0:T(8,128)(2,1)} %get-tuple-element.183), channel_id=1, source_target_pairs={{0,8},{4,12},{8,0},{12,4},{16,24},{20,28},{24,16},{28,20},{1,9},{5... | collective-permute-start | bytes 1327112 | tf_op jit(solution)/shard_map/ppermute | solution.py:39
  231.7 20.8 %collective-permute-start.23 = (bf16[4,48,1152]{2,1,0:T(8,128)(2,1)}, bf16[4,48,1152]{2,1,0:T(8,128)(2,1)S(1)}, u32[]{:S(2)}, u32[]{:S(2)}) collective-permute-start(bf16[4,48,1152]{2,1,0:T(8,128)(2,1)} %get-tuple-element.185), channel_id=1, source_target_pairs={{0,16},{4,20},{8,24},{12,28},{16,0},{20,4},{24,8},{28,12},{1,17},{... | collective-permute-start | bytes 1327112 | tf_op jit(solution)/shard_map/ppermute | solution.py:39
  233.2 20.9 %collective-permute-start.24 = (bf16[4,48,1152]{2,1,0:T(8,128)(2,1)}, bf16[4,48,1152]{2,1,0:T(8,128)(2,1)}, u32[]{:S(2)}, u32[]{:S(2)}) collective-permute-start(bf16[4,48,1152]{2,1,0:T(8,128)(2,1)} %get-tuple-element.184), channel_id=1, source_target_pairs={{0,24},{4,28},{8,16},{12,20},{16,8},{20,12},{24,0},{28,4},{1,25},{... | collective-permute-start | bytes 1327112 | tf_op jit(solution)/shard_map/ppermute | solution.py:39
  235.0 22.1 %collective-permute-start.26 = (bf16[2,48,2304]{2,1,0:T(8,128)(2,1)}, bf16[2,48,2304]{2,1,0:T(8,128)(2,1)S(1)}, u32[]{:S(2)}, u32[]{:S(2)}) collective-permute-start(bf16[2,48,2304]{2,1,0:T(8,128)(2,1)} %constant_dynamic-slice_fusion.1), channel_id=1, source_target_pairs={{0,2},{1,3},{2,0},{3,1},{4,6},{5,7},{6,4},{7,5},{8,10},{9,11},{10,... | collective-permute-start | bytes 1327112 | tf_op jit(solution)/shard_map/ppermute | solution.py:39
  257.2 10.7 %collective-permute-start.27 = (bf16[1,48,2304]{2,1,0:T(8,128)(2,1)S(1)}, bf16[1,48,2304]{2,1,0:T(8,128)(2,1)S(1)}, u32[]{:S(2)}, u32[]{:S(2)}) collective-permute-start(bf16[1,48,2304]{2,1,0:T(8,128)(2,1)S(1)} %constant_dynamic-slice_fusion), channel_id=1, source_target_pairs={{0,1},{1,0},{2,3},{3,2},{4,5},{5,4},{6,7},{7,6},{8,9},{9,8},{10,11... | collective-permute-start | bytes 663560 | tf_op jit(solution)/shard_map/ppermute | solution.py:39
  257.4 14.4 %collective-permute-start.25 = (bf16[48,1152]{1,0:T(8,128)(2,1)S(1)}, bf16[48,1152]{1,0:T(8,128)(2,1)S(1)}, u32[]{:S(2)}, u32[]{:S(2)}) collective-permute-start(bf16[48,1152]{1,0:T(8,128)(2,1)S(1)} %get-tuple-element.192), channel_id=1, source_target_pairs={{0,1},{1,0},{2,3},{3,2},{4,5},{5,4},{6,7},{7,6},{8,9},{9,8},{10,11... | collective-permute-start | bytes 331784 | tf_op jit(solution)/shard_map/ppermute | solution.py:39
  259.4 12.3 %collective-permute-start.28 = (bf16[48,1152]{1,0:T(8,128)(2,1)S(1)}, bf16[48,1152]{1,0:T(8,128)(2,1)S(1)}, u32[]{:S(2)}, u32[]{:S(2)}) collective-permute-start(bf16[48,1152]{1,0:T(8,128)(2,1)S(1)} %get-tuple-element.194), channel_id=1, source_target_pairs={{0,2},{1,3},{2,0},{3,1},{4,6},{5,7},{6,4},{7,5},{8,10},{9,11},{10,... | collective-permute-start | bytes 331784 | tf_op jit(solution)/shard_map/ppermute | solution.py:39
  259.4 12.3 %collective-permute-start.29 = (bf16[48,1152]{1,0:T(8,128)(2,1)S(1)}, bf16[48,1152]{1,0:T(8,128)(2,1)S(1)}, u32[]{:S(2)}, u32[]{:S(2)}) collective-permute-start(bf16[48,1152]{1,0:T(8,128)(2,1)S(1)} %get-tuple-element.193), channel_id=1, source_target_pairs={{0,3},{1,2},{2,1},{3,0},{4,7},{5,6},{6,5},{7,4},{8,11},{9,10},{10,... | collective-permute-start | bytes 331784 | tf_op jit(solution)/shard_map/ppermute | solution.py:39
  269.6 11.7 %collective-permute-start.32 = (bf16[48,2304]{1,0:T(8,128)(2,1)S(1)}, bf16[48,2304]{1,0:T(8,128)(2,1)S(1)}, u32[]{:S(2)}, u32[]{:S(2)}) collective-permute-start(bf16[48,2304]{1,0:T(8,128)(2,1)S(1)} %fusion.23), channel_id=1, source_target_pairs={{0,16},{4,20},{8,24},{12,28},{16,0},{20,4},{24,8},{28,12},{1,17},{... | collective-permute-start | bytes 663560 | tf_op jit(solution)/shard_map/ppermute | solution.py:39
  271.8 9.9 %collective-permute-start.31 = (bf16[48,2304]{1,0:T(8,128)(2,1)S(1)}, bf16[48,2304]{1,0:T(8,128)(2,1)S(1)}, u32[]{:S(2)}, u32[]{:S(2)}) collective-permute-start(bf16[48,2304]{1,0:T(8,128)(2,1)S(1)} %fusion.23), channel_id=1, source_target_pairs={{0,8},{4,12},{8,0},{12,4},{16,24},{20,28},{24,16},{28,20},{1,9},{5... | collective-permute-start | bytes 663560 | tf_op jit(solution)/shard_map/ppermute | solution.py:39
  271.9 11.1 %collective-permute-start.35 = (bf16[48,1152]{1,0:T(8,128)(2,1)S(1)}, bf16[48,1152]{1,0:T(8,128)(2,1)S(1)}, u32[]{:S(2)}, u32[]{:S(2)}) collective-permute-start(bf16[48,1152]{1,0:T(8,128)(2,1)S(1)} %get-tuple-element.173), channel_id=1, source_target_pairs={{0,24},{4,28},{8,16},{12,20},{16,8},{20,12},{24,0},{28,4},{1,25},{... | collective-permute-start | bytes 331784 | tf_op jit(solution)/shard_map/ppermute | solution.py:39
  273.4 10.6 %collective-permute-start.34 = (bf16[48,1152]{1,0:T(8,128)(2,1)S(1)}, bf16[48,1152]{1,0:T(8,128)(2,1)S(1)}, u32[]{:S(2)}, u32[]{:S(2)}) collective-permute-start(bf16[48,1152]{1,0:T(8,128)(2,1)S(1)} %get-tuple-element.173), channel_id=1, source_target_pairs={{0,16},{4,20},{8,24},{12,28},{16,0},{20,4},{24,8},{28,12},{1,17},{... | collective-permute-start | bytes 331784 | tf_op jit(solution)/shard_map/ppermute | solution.py:39
  284.2 10.4 %collective-permute-start.36 = (bf16[192,1152]{1,0:T(8,128)(2,1)S(1)}, bf16[192,1152]{1,0:T(8,128)(2,1)S(1)}, u32[]{:S(2)}, u32[]{:S(2)}) collective-permute-start(bf16[192,1152]{1,0:T(8,128)(2,1)S(1)} %bitcast.85), channel_id=1, source_target_pairs={{0,4},{4,0},{8,12},{12,8},{16,20},{20,16},{24,28},{28,24},{1,5},{5... | collective-permute-start | bytes 1327112 | tf_op jit(solution)/shard_map/ppermute | solution.py:39
  (33 other events, 156.7 us)
